TPU v7x, 256 devices: a whole 4x4x8 slice. The times are simulated.
256 devices in a mesh: tm: 4 (over z_hi, core), space: 64 (over x, y, z_lo).
Axes of the slice: x: 4, y: 4, z: 8 (z_hi: 2, z_lo: 4; z = z_hi * 4 + z_lo), core: 2. Of those that a mesh axis runs over, the one named last changes fastest.
Arguments:
- grain_labels: int32 [256, 16, 256], P('space'), may hold values from 0 to 127
- particle_mask: int32 [256, 16, 256], P('space'), may hold values 0 or 1
- grain_class: int32 [128], replicated, may hold values from 0 to 3
- class_energy: float32 [4], replicated, may hold values from 0.1 to 1
Outputs:
- slice_start: float32 [4, 8, 256, 16, 256], P('tm', None, 'space')
- slice_end: float32 [4, 8, 256, 16, 256], P('tm', None, 'space')
All inputs are finite; a program needn't handle non-finite values. No bound on the sum of `particle_mask` on one device may be relied on, other than what follows from the above.
Results may differ from a plain program's by a relative error of at most 0.0001.
Values sent between devices are 32-bit elements; how exact they have to be, the bound alone decides.
A program may use at most 64 MiB of HBM per device.

v0:
```python
import jax
import jax.numpy as jnp
from jax import lax
from jax.sharding import PartitionSpec as P

ORDERS = 8
FINE = 2
ITERS = 2


fine_dt = 0.06


def padded_2(shard, sides, width):
    for axis, dim in sides:
        peers, length = (lax.axis_size(axis), shard.shape[dim])
        up = [(i, (i + 1) % peers) for i in range(peers)]
        down = [(j, i) for i, j in up]
        last = lax.slice_in_dim(shard, length - width, length, axis=dim)
        first = lax.slice_in_dim(shard, 0, width, axis=dim)
        before = lax.ppermute(last, axis, up)
        after = lax.ppermute(first, axis, down)
        shard = jnp.concatenate([before, shard, after], axis=dim)
    return shard


def from_behind(block, axis, distance):
    devices = range(lax.axis_size(axis))
    route = [(i - distance, i) for i in devices if i - distance in devices]
    return lax.ppermute(block, axis, route)


def coefficients(labels, particles, grain_class, class_energy):
    grain_energy = jnp.take(class_energy, grain_class)
    stored = jnp.take(grain_energy, labels)
    orders = jnp.arange(ORDERS, dtype=jnp.int32)[:, None, None, None]
    own = (labels[None] % ORDERS == orders).astype(jnp.float32)
    drive = stored[None] * own
    mobility = 1.0 - 0.75 * particles.astype(jnp.float32)
    return (own, drive, mobility)


def evolve(center, xplus, xminus, drive, mobility, step_size):
    beside = xplus + xminus + jnp.roll(center, -1, 2) + jnp.roll(center, 1, 2)
    beside = beside + jnp.roll(center, -1, 3) + jnp.roll(center, 1, 3)
    laplace = beside - 6.0 * center
    squares = center * center
    total = jnp.sum(squares, axis=0, keepdims=True)
    force = squares * center - center + 3.0 * center * (total - squares) - laplace + drive * center
    return center - step_size * mobility[None] * force


def advance(field, drive, mobility, step_size):
    padded = padded_2(field, (("space", 1),), 1)
    return evolve(padded[:, 1:-1], padded[:, 2:], padded[:, :-2], drive, mobility, step_size)


def local(grain_labels, particle_mask, grain_class, class_energy):
    own, drive, mobility = coefficients(grain_labels, particle_mask, grain_class, class_energy)
    coarse_dt = fine_dt * FINE
    slices = lax.axis_size("tm")
    first = lax.axis_index("tm") == 0

    def coarse(field):
        return advance(field, drive, mobility, coarse_dt)

    def passing(ending):
        return from_behind(ending, "tm", 1)

    current = own
    latest = coarse(current)
    ending = latest
    for turn in range(slices - 1):
        current = jnp.where(first, own, passing(ending))
        latest = coarse(current)
        ending = latest
    for sweep in range(ITERS):
        fine_field = current
        for inner in range(FINE):
            fine_field = advance(fine_field, drive, mobility, fine_dt)
        jump = fine_field - latest
        ending = fine_field
        for turn in range(slices - 1):
            current = jnp.where(first, own, passing(ending))
            latest = coarse(current)
            ending = latest + jump
    return (current[None], ending[None])


def solution(mesh):
    placed = (P("space", None, None), P("space", None, None), P(), P())
    return jax.shard_map(
        local,
        mesh=mesh,
        in_specs=placed,
        out_specs=(P("tm", None, "space", None, None), P("tm", None, "space", None, None)),
        check_vma=False,
    )
```

profile of v0, /device:TPU:1, one launch (start us, length us, event | category | flops | bytes accessed | tf_op | source)
XLA Modules:
  0.0 405.2 jit_solution(11500010255483664283)
XLA Ops:
  0.6 0.9 compare_select_fusion
  2.3 9.8 %collective-permute-start = (f32[8,1,16,256]{3,2,1,0:T(8,128)}, f32[8,1,16,256]{3,2,1,0:T(8,128)}, u32[]{:S(2)}, u32[]{:S(2)}) collective-permute-start(f32[8,1,16,256]{3,2,1,0:T(8,128)} %get-tuple-element.146), channel_id=1, source_target_pairs={{1,0},{2,1},{3,2},{4,3},{5,4},{6,5},{7,6},{8,7},{9,8},{10,9},{11,1... | collective-permute-start | bytes 393224 | tf_op jit(solution)/shard_map/ppermute | solution.py:22
  14.3 2.4 and_select_fusion.1
  16.7 97.2 %gather_fusion = f32[16384]{0:T(1024)S(1)} fusion(f32[128]{0:T(128)S(1)} %and_select_fusion.1, s32[16384]{0:T(1024)S(1)} %broadcast_clamp_fusion), kind=kCustom, calls=%fused_computation | custom fusion | bytes 196608 | tf_op jit(solution)/shard_map/jit(_take)/gather | solution.py:35
  114.8 0.9 fusion.150
  115.8 2.4 convert_subtract_fusion
  118.2 6.9 %collective-permute-start.2 = (f32[8,4,16,256]{3,2,1,0:T(8,128)}, f32[8,4,16,256]{3,2,1,0:T(8,128)S(1)}, u32[]{:S(2)}, u32[]{:S(2)}) collective-permute-start(f32[8,4,16,256]{3,2,1,0:T(8,128)} %convert_subtract_fusion), channel_id=1, source_target_pairs={{0,64},{64,128},{128,192},{1,65},{65,129},{129,193},{2,66},{66,130... | collective-permute-start | bytes 1572872 | tf_op jit(solution)/shard_map/ppermute | solution.py:30
  125.1 6.4 %collective-permute-done.2 = f32[8,4,16,256]{3,2,1,0:T(8,128)S(1)} collective-permute-done((f32[8,4,16,256]{3,2,1,0:T(8,128)}, f32[8,4,16,256]{3,2,1,0:T(8,128)S(1)}, u32[]{:S(2)}, u32[]{:S(2)}) %collective-permute-start.2) | collective-permute-done | bytes 524320 | tf_op jit(solution)/shard_map/ppermute | solution.py:30
  132.1 7.8 %collective-permute-start.3 = (f32[8,1,16,256]{3,2,1,0:T(8,128)S(1)}, f32[8,1,16,256]{3,2,1,0:T(8,128)S(1)}, u32[]{:S(2)}, u32[]{:S(2)}) collective-permute-start(f32[8,1,16,256]{3,2,1,0:T(8,128)S(1)} %get-tuple-element.136), channel_id=1, source_target_pairs={{1,0},{2,1},{3,2},{4,3},{5,4},{6,5},{7,6},{8,7},{9,8},{10,9},{11,1... | collective-permute-start | bytes 393224 | tf_op jit(solution)/shard_map/ppermute | solution.py:22
  140.0 1.9 collective-permute-done.3
  141.9 7.9 %collective-permute-done.4 = f32[8,1,16,256]{3,2,1,0:T(8,128)S(1)} collective-permute-done((f32[8,1,16,256]{3,2,1,0:T(8,128)S(1)}, f32[8,1,16,256]{3,2,1,0:T(8,128)S(1)}, u32[]{:S(2)}, u32[]{:S(2)}) %collective-permute-start.4) | collective-permute-done | bytes 131104 | tf_op jit(solution)/shard_map/ppermute | solution.py:21
  150.4 9.7 %collective-permute-start.5 = (f32[8,4,16,256]{3,2,1,0:T(8,128)S(1)}, f32[8,4,16,256]{3,2,1,0:T(8,128)S(1)}, u32[]{:S(2)}, u32[]{:S(2)}) collective-permute-start(f32[8,4,16,256]{3,2,1,0:T(8,128)S(1)} %fusion.8), channel_id=1, source_target_pairs={{0,64},{64,128},{128,192},{1,65},{65,129},{129,193},{2,66},{66,130... | collective-permute-start | bytes 1572872 | tf_op jit(solution)/shard_map/ppermute | solution.py:30
  160.1 6.1 %collective-permute-done.5 = f32[8,4,16,256]{3,2,1,0:T(8,128)S(1)} collective-permute-done((f32[8,4,16,256]{3,2,1,0:T(8,128)S(1)}, f32[8,4,16,256]{3,2,1,0:T(8,128)S(1)}, u32[]{:S(2)}, u32[]{:S(2)}) %collective-permute-start.5) | collective-permute-done | bytes 524320 | tf_op jit(solution)/shard_map/ppermute | solution.py:30
  166.8 1.2 collective-permute-start.6
  168.0 1.1 collective-permute-start.7
  169.2 2.2 collective-permute-done.6
  171.4 6.4 %collective-permute-done.7 = f32[8,1,16,256]{3,2,1,0:T(8,128)S(1)} collective-permute-done((f32[8,1,16,256]{3,2,1,0:T(8,128)S(1)}, f32[8,1,16,256]{3,2,1,0:T(8,128)S(1)}, u32[]{:S(2)}, u32[]{:S(2)}) %collective-permute-start.7) | collective-permute-done | bytes 131104 | tf_op jit(solution)/shard_map/ppermute | solution.py:21
  178.4 9.8 %collective-permute-start.8 = (f32[8,4,16,256]{3,2,1,0:T(8,128)S(1)}, f32[8,4,16,256]{3,2,1,0:T(8,128)S(1)}, u32[]{:S(2)}, u32[]{:S(2)}) collective-permute-start(f32[8,4,16,256]{3,2,1,0:T(8,128)S(1)} %fusion.14), channel_id=1, source_target_pairs={{0,64},{64,128},{128,192},{1,65},{65,129},{129,193},{2,66},{66,130... | collective-permute-start | bytes 1572872 | tf_op jit(solution)/shard_map/ppermute | solution.py:30
  188.3 6.1 %collective-permute-done.8 = f32[8,4,16,256]{3,2,1,0:T(8,128)S(1)} collective-permute-done((f32[8,4,16,256]{3,2,1,0:T(8,128)S(1)}, f32[8,4,16,256]{3,2,1,0:T(8,128)S(1)}, u32[]{:S(2)}, u32[]{:S(2)}) %collective-permute-start.8) | collective-permute-done | bytes 524320 | tf_op jit(solution)/shard_map/ppermute | solution.py:30
  194.9 1.4 collective-permute-start.9
  196.3 3.7 collective-permute-start.10
  200.1 4.9 %collective-permute-done.9 = f32[8,1,16,256]{3,2,1,0:T(8,128)S(1)} collective-permute-done((f32[8,1,16,256]{3,2,1,0:T(8,128)S(1)}, f32[8,1,16,256]{3,2,1,0:T(8,128)S(1)}, u32[]{:S(2)}, u32[]{:S(2)}) %collective-permute-start.9) | collective-permute-done | bytes 131104 | tf_op jit(solution)/shard_map/ppermute | solution.py:22
  205.0 4.3 %collective-permute-done.10 = f32[8,1,16,256]{3,2,1,0:T(8,128)S(1)} collective-permute-done((f32[8,1,16,256]{3,2,1,0:T(8,128)S(1)}, f32[8,1,16,256]{3,2,1,0:T(8,128)S(1)}, u32[]{:S(2)}, u32[]{:S(2)}) %collective-permute-start.10) | collective-permute-done | bytes 131104 | tf_op jit(solution)/shard_map/ppermute | solution.py:21
  210.7 1.5 collective-permute-start.12
  212.2 3.3 collective-permute-done.11
  215.4 5.1 %collective-permute-done.12 = f32[8,1,16,256]{3,2,1,0:T(8,128)S(1)} collective-permute-done((f32[8,1,16,256]{3,2,1,0:T(8,128)S(1)}, f32[8,1,16,256]{3,2,1,0:T(8,128)S(1)}, u32[]{:S(2)}, u32[]{:S(2)}) %collective-permute-start.12) | collective-permute-done | bytes 131104 | tf_op jit(solution)/shard_map/ppermute | solution.py:21
  221.2 10.7 %collective-permute-start.13 = (f32[8,4,16,256]{3,2,1,0:T(8,128)S(1)}, f32[8,4,16,256]{3,2,1,0:T(8,128)S(1)}, u32[]{:S(2)}, u32[]{:S(2)}) collective-permute-start(f32[8,4,16,256]{3,2,1,0:T(8,128)S(1)} %fusion.24), channel_id=1, source_target_pairs={{0,64},{64,128},{128,192},{1,65},{65,129},{129,193},{2,66},{66,130... | collective-permute-start | bytes 1572872 | tf_op jit(solution)/shard_map/ppermute | solution.py:30
  231.9 6.1 %collective-permute-done.13 = f32[8,4,16,256]{3,2,1,0:T(8,128)S(1)} collective-permute-done((f32[8,4,16,256]{3,2,1,0:T(8,128)S(1)}, f32[8,4,16,256]{3,2,1,0:T(8,128)S(1)}, u32[]{:S(2)}, u32[]{:S(2)}) %collective-permute-start.13) | collective-permute-done | bytes 524320 | tf_op jit(solution)/shard_map/ppermute | solution.py:30
  238.6 1.2 collective-permute-start.14
  240.4 2.2 collective-permute-done.14
  242.6 7.0 %collective-permute-done.15 = f32[8,1,16,256]{3,2,1,0:T(8,128)S(1)} collective-permute-done((f32[8,1,16,256]{3,2,1,0:T(8,128)S(1)}, f32[8,1,16,256]{3,2,1,0:T(8,128)S(1)}, u32[]{:S(2)}, u32[]{:S(2)}) %collective-permute-start.15) | collective-permute-done | bytes 131104 | tf_op jit(solution)/shard_map/ppermute | solution.py:21
  250.3 9.8 %collective-permute-start.16 = (f32[8,4,16,256]{3,2,1,0:T(8,128)S(1)}, f32[8,4,16,256]{3,2,1,0:T(8,128)S(1)}, u32[]{:S(2)}, u32[]{:S(2)}) collective-permute-start(f32[8,4,16,256]{3,2,1,0:T(8,128)S(1)} %fusion.31), channel_id=1, source_target_pairs={{0,64},{64,128},{128,192},{1,65},{65,129},{129,193},{2,66},{66,130... | collective-permute-start | bytes 1572872 | tf_op jit(solution)/shard_map/ppermute | solution.py:30
  260.2 6.1 %collective-permute-done.16 = f32[8,4,16,256]{3,2,1,0:T(8,128)S(1)} collective-permute-done((f32[8,4,16,256]{3,2,1,0:T(8,128)S(1)}, f32[8,4,16,256]{3,2,1,0:T(8,128)S(1)}, u32[]{:S(2)}, u32[]{:S(2)}) %collective-permute-start.16) | collective-permute-done | bytes 524320 | tf_op jit(solution)/shard_map/ppermute | solution.py:30
  266.8 1.3 collective-permute-start.17
  268.1 2.4 collective-permute-start.18
  270.6 2.2 collective-permute-done.17
  272.8 5.1 %collective-permute-done.18 = f32[8,1,16,256]{3,2,1,0:T(8,128)S(1)} collective-permute-done((f32[8,1,16,256]{3,2,1,0:T(8,128)S(1)}, f32[8,1,16,256]{3,2,1,0:T(8,128)S(1)}, u32[]{:S(2)}, u32[]{:S(2)}) %collective-permute-start.18) | collective-permute-done | bytes 131104 | tf_op jit(solution)/shard_map/ppermute | solution.py:21
  278.7 9.9 %collective-permute-start.19 = (f32[8,4,16,256]{3,2,1,0:T(8,128)S(1)}, f32[8,4,16,256]{3,2,1,0:T(8,128)S(1)}, u32[]{:S(2)}, u32[]{:S(2)}) collective-permute-start(f32[8,4,16,256]{3,2,1,0:T(8,128)S(1)} %fusion.38), channel_id=1, source_target_pairs={{0,64},{64,128},{128,192},{1,65},{65,129},{129,193},{2,66},{66,130... | collective-permute-start | bytes 1572872 | tf_op jit(solution)/shard_map/ppermute | solution.py:30
  288.5 6.1 %collective-permute-done.19 = f32[8,4,16,256]{3,2,1,0:T(8,128)S(1)} collective-permute-done((f32[8,4,16,256]{3,2,1,0:T(8,128)S(1)}, f32[8,4,16,256]{3,2,1,0:T(8,128)S(1)}, u32[]{:S(2)}, u32[]{:S(2)}) %collective-permute-start.19) | collective-permute-done | bytes 524320 | tf_op jit(solution)/shard_map/ppermute | solution.py:30
  295.2 1.3 collective-permute-start.20
  296.5 6.5 %collective-permute-start.21 = (f32[8,1,16,256]{3,2,1,0:T(8,128)S(1)}, f32[8,1,16,256]{3,2,1,0:T(8,128)S(1)}, u32[]{:S(2)}, u32[]{:S(2)}) collective-permute-start(f32[8,1,16,256]{3,2,1,0:T(8,128)S(1)} %get-tuple-element.69), channel_id=1, source_target_pairs={{0,1},{1,2},{2,3},{3,4},{4,5},{5,6},{6,7},{7,8},{8,9},{9,10},{10,1... | collective-permute-start | bytes 393224 | tf_op jit(solution)/shard_map/ppermute | solution.py:21
  303.1 3.2 collective-permute-done.20
  307.9 1.1 collective-permute-start.23
  309.1 2.3 collective-permute-done.22
  311.4 6.4 %collective-permute-done.23 = f32[8,1,16,256]{3,2,1,0:T(8,128)S(1)} collective-permute-done((f32[8,1,16,256]{3,2,1,0:T(8,128)S(1)}, f32[8,1,16,256]{3,2,1,0:T(8,128)S(1)}, u32[]{:S(2)}, u32[]{:S(2)}) %collective-permute-start.23) | collective-permute-done | bytes 131104 | tf_op jit(solution)/shard_map/ppermute | solution.py:21
  318.4 11.4 %collective-permute-start.24 = (f32[8,4,16,256]{3,2,1,0:T(8,128)S(1)}, f32[8,4,16,256]{3,2,1,0:T(8,128)S(1)}, u32[]{:S(2)}, u32[]{:S(2)}) collective-permute-start(f32[8,4,16,256]{3,2,1,0:T(8,128)S(1)} %fusion.48), channel_id=1, source_target_pairs={{0,64},{64,128},{128,192},{1,65},{65,129},{129,193},{2,66},{66,130... | collective-permute-start | bytes 1572872 | tf_op jit(solution)/shard_map/ppermute | solution.py:30
  329.8 6.1 %collective-permute-done.24 = f32[8,4,16,256]{3,2,1,0:T(8,128)S(1)} collective-permute-done((f32[8,4,16,256]{3,2,1,0:T(8,128)S(1)}, f32[8,4,16,256]{3,2,1,0:T(8,128)S(1)}, u32[]{:S(2)}, u32[]{:S(2)}) %collective-permute-start.24) | collective-permute-done | bytes 524320 | tf_op jit(solution)/shard_map/ppermute | solution.py:30
  336.5 1.0 collective-permute-start.25
  337.5 2.7 collective-permute-start.26
  340.3 2.2 collective-permute-done.25
  342.5 4.8 %collective-permute-done.26 = f32[8,1,16,256]{3,2,1,0:T(8,128)S(1)} collective-permute-done((f32[8,1,16,256]{3,2,1,0:T(8,128)S(1)}, f32[8,1,16,256]{3,2,1,0:T(8,128)S(1)}, u32[]{:S(2)}, u32[]{:S(2)}) %collective-permute-start.26) | collective-permute-done | bytes 131104 | tf_op jit(solution)/shard_map/ppermute | solution.py:21
  348.0 9.8 %collective-permute-start.27 = (f32[8,4,16,256]{3,2,1,0:T(8,128)S(1)}, f32[8,4,16,256]{3,2,1,0:T(8,128)S(1)}, u32[]{:S(2)}, u32[]{:S(2)}) collective-permute-start(f32[8,4,16,256]{3,2,1,0:T(8,128)S(1)} %get-tuple-element.6), channel_id=1, source_target_pairs={{0,64},{64,128},{128,192},{1,65},{65,129},{129,193},{2,66},{66,130... | collective-permute-start | bytes 1572872 | tf_op jit(solution)/shard_map/ppermute | solution.py:30
  357.9 6.1 %collective-permute-done.27 = f32[8,4,16,256]{3,2,1,0:T(8,128)S(1)} collective-permute-done((f32[8,4,16,256]{3,2,1,0:T(8,128)S(1)}, f32[8,4,16,256]{3,2,1,0:T(8,128)S(1)}, u32[]{:S(2)}, u32[]{:S(2)}) %collective-permute-start.27) | collective-permute-done | bytes 524320 | tf_op jit(solution)/shard_map/ppermute | solution.py:30
  364.5 1.2 collective-permute-start.28
  365.8 4.1 %collective-permute-start.29 = (f32[8,1,16,256]{3,2,1,0:T(8,128)S(1)}, f32[8,1,16,256]{3,2,1,0:T(8,128)S(1)}, u32[]{:S(2)}, u32[]{:S(2)}) collective-permute-start(f32[8,1,16,256]{3,2,1,0:T(8,128)S(1)} %get-tuple-element.47), channel_id=1, source_target_pairs={{0,1},{1,2},{2,3},{3,4},{4,5},{5,6},{6,7},{7,8},{8,9},{9,10},{10,1... | collective-permute-start | bytes 393224 | tf_op jit(solution)/shard_map/ppermute | solution.py:21
  369.9 2.2 collective-permute-done.28
  372.1 3.5 collective-permute-done.29
  376.2 9.8 %collective-permute-start.30 = (f32[8,4,16,256]{3,2,1,0:T(8,128)S(1)}, f32[8,4,16,256]{3,2,1,0:T(8,128)S(1)}, u32[]{:S(2)}, u32[]{:S(2)}) collective-permute-start(f32[8,4,16,256]{3,2,1,0:T(8,128)S(1)} %fusion.62), channel_id=1, source_target_pairs={{0,64},{64,128},{128,192},{1,65},{65,129},{129,193},{2,66},{66,130... | collective-permute-start | bytes 1572872 | tf_op jit(solution)/shard_map/ppermute | solution.py:30
  386.1 6.1 %collective-permute-done.30 = f32[8,4,16,256]{3,2,1,0:T(8,128)S(1)} collective-permute-done((f32[8,4,16,256]{3,2,1,0:T(8,128)S(1)}, f32[8,4,16,256]{3,2,1,0:T(8,128)S(1)}, u32[]{:S(2)}, u32[]{:S(2)}) %collective-permute-start.30) | collective-permute-done | bytes 524320 | tf_op jit(solution)/shard_map/ppermute | solution.py:30
  392.7 1.2 collective-permute-start.31
  393.9 4.5 %collective-permute-start.32 = (f32[8,1,16,256]{3,2,1,0:T(8,128)S(1)}, f32[8,1,16,256]{3,2,1,0:T(8,128)S(1)}, u32[]{:S(2)}, u32[]{:S(2)}) collective-permute-start(f32[8,1,16,256]{3,2,1,0:T(8,128)S(1)} %get-tuple-element.37), channel_id=1, source_target_pairs={{0,1},{1,2},{2,3},{3,4},{4,5},{5,6},{6,7},{7,8},{8,9},{9,10},{10,1... | collective-permute-start | bytes 393224 | tf_op jit(solution)/shard_map/ppermute | solution.py:21
  398.5 2.2 collective-permute-done.31
  400.7 3.1 collective-permute-done.32
  403.8 1.4 fusion.70
  (101 shorter events, 18.1 us)
Async XLA Ops:
  2.3 113.5 %collective-permute-start = (f32[8,1,16,256]{3,2,1,0:T(8,128)}, f32[8,1,16,256]{3,2,1,0:T(8,128)}, u32[]{:S(2)}, u32[]{:S(2)}) collective-permute-start(f32[8,1,16,256]{3,2,1,0:T(8,128)} %get-tuple-element.146), channel_id=1, source_target_pairs={{1,0},{2,1},{3,2},{4,3},{5,4},{6,5},{7,6},{8,7},{9,8},{10,9},{11,1... | collective-permute-start | bytes 393224 | tf_op jit(solution)/shard_map/ppermute | solution.py:22
  12.1 103.7 %collective-permute-start.1 = (f32[8,1,16,256]{3,2,1,0:T(8,128)}, f32[8,1,16,256]{3,2,1,0:T(8,128)}, u32[]{:S(2)}, u32[]{:S(2)}) collective-permute-start(f32[8,1,16,256]{3,2,1,0:T(8,128)} %get-tuple-element.147), channel_id=1, source_target_pairs={{0,1},{1,2},{2,3},{3,4},{4,5},{5,6},{6,7},{7,8},{8,9},{9,10},{10,1... | collective-permute-start | bytes 393224 | tf_op jit(solution)/shard_map/ppermute | solution.py:21
  12.3 0.7 copy-start.2
  13.7 0.7 copy-start.3
  113.9 0.8 copy-start.1
  118.2 13.4 %collective-permute-start.2 = (f32[8,4,16,256]{3,2,1,0:T(8,128)}, f32[8,4,16,256]{3,2,1,0:T(8,128)S(1)}, u32[]{:S(2)}, u32[]{:S(2)}) collective-permute-start(f32[8,4,16,256]{3,2,1,0:T(8,128)} %convert_subtract_fusion), channel_id=1, source_target_pairs={{0,64},{64,128},{128,192},{1,65},{65,129},{129,193},{2,66},{66,130... | collective-permute-start | bytes 1572872 | tf_op jit(solution)/shard_map/ppermute | solution.py:30
  132.1 9.8 %collective-permute-start.3 = (f32[8,1,16,256]{3,2,1,0:T(8,128)S(1)}, f32[8,1,16,256]{3,2,1,0:T(8,128)S(1)}, u32[]{:S(2)}, u32[]{:S(2)}) collective-permute-start(f32[8,1,16,256]{3,2,1,0:T(8,128)S(1)} %get-tuple-element.136), channel_id=1, source_target_pairs={{1,0},{2,1},{3,2},{4,3},{5,4},{6,5},{7,6},{8,7},{9,8},{10,9},{11,1... | collective-permute-start | bytes 393224 | tf_op jit(solution)/shard_map/ppermute | solution.py:22
  139.9 9.8 %collective-permute-start.4 = (f32[8,1,16,256]{3,2,1,0:T(8,128)S(1)}, f32[8,1,16,256]{3,2,1,0:T(8,128)S(1)}, u32[]{:S(2)}, u32[]{:S(2)}) collective-permute-start(f32[8,1,16,256]{3,2,1,0:T(8,128)S(1)} %get-tuple-element.137), channel_id=1, source_target_pairs={{0,1},{1,2},{2,3},{3,4},{4,5},{5,6},{6,7},{7,8},{8,9},{9,10},{10,1... | collective-permute-start | bytes 393224 | tf_op jit(solution)/shard_map/ppermute | solution.py:21
  150.4 15.8 %collective-permute-start.5 = (f32[8,4,16,256]{3,2,1,0:T(8,128)S(1)}, f32[8,4,16,256]{3,2,1,0:T(8,128)S(1)}, u32[]{:S(2)}, u32[]{:S(2)}) collective-permute-start(f32[8,4,16,256]{3,2,1,0:T(8,128)S(1)} %fusion.8), channel_id=1, source_target_pairs={{0,64},{64,128},{128,192},{1,65},{65,129},{129,193},{2,66},{66,130... | collective-permute-start | bytes 1572872 | tf_op jit(solution)/shard_map/ppermute | solution.py:30
  166.8 4.6 %collective-permute-start.6 = (f32[8,1,16,256]{3,2,1,0:T(8,128)S(1)}, f32[8,1,16,256]{3,2,1,0:T(8,128)S(1)}, u32[]{:S(2)}, u32[]{:S(2)}) collective-permute-start(f32[8,1,16,256]{3,2,1,0:T(8,128)S(1)} %get-tuple-element.126), channel_id=1, source_target_pairs={{1,0},{2,1},{3,2},{4,3},{5,4},{6,5},{7,6},{8,7},{9,8},{10,9},{11,1... | collective-permute-start | bytes 393224 | tf_op jit(solution)/shard_map/ppermute | solution.py:22
  168.0 9.8 %collective-permute-start.7 = (f32[8,1,16,256]{3,2,1,0:T(8,128)S(1)}, f32[8,1,16,256]{3,2,1,0:T(8,128)S(1)}, u32[]{:S(2)}, u32[]{:S(2)}) collective-permute-start(f32[8,1,16,256]{3,2,1,0:T(8,128)S(1)} %get-tuple-element.127), channel_id=1, source_target_pairs={{0,1},{1,2},{2,3},{3,4},{4,5},{5,6},{6,7},{7,8},{8,9},{9,10},{10,1... | collective-permute-start | bytes 393224 | tf_op jit(solution)/shard_map/ppermute | solution.py:21
  178.4 15.9 %collective-permute-start.8 = (f32[8,4,16,256]{3,2,1,0:T(8,128)S(1)}, f32[8,4,16,256]{3,2,1,0:T(8,128)S(1)}, u32[]{:S(2)}, u32[]{:S(2)}) collective-permute-start(f32[8,4,16,256]{3,2,1,0:T(8,128)S(1)} %fusion.14), channel_id=1, source_target_pairs={{0,64},{64,128},{128,192},{1,65},{65,129},{129,193},{2,66},{66,130... | collective-permute-start | bytes 1572872 | tf_op jit(solution)/shard_map/ppermute | solution.py:30
  194.9 10.1 %collective-permute-start.9 = (f32[8,1,16,256]{3,2,1,0:T(8,128)S(1)}, f32[8,1,16,256]{3,2,1,0:T(8,128)S(1)}, u32[]{:S(2)}, u32[]{:S(2)}) collective-permute-start(f32[8,1,16,256]{3,2,1,0:T(8,128)S(1)} %get-tuple-element.108), channel_id=1, source_target_pairs={{1,0},{2,1},{3,2},{4,3},{5,4},{6,5},{7,6},{8,7},{9,8},{10,9},{11,1... | collective-permute-start | bytes 393224 | tf_op jit(solution)/shard_map/ppermute | solution.py:22
  196.3 13.0 %collective-permute-start.10 = (f32[8,1,16,256]{3,2,1,0:T(8,128)S(1)}, f32[8,1,16,256]{3,2,1,0:T(8,128)S(1)}, u32[]{:S(2)}, u32[]{:S(2)}) collective-permute-start(f32[8,1,16,256]{3,2,1,0:T(8,128)S(1)} %get-tuple-element.109), channel_id=1, source_target_pairs={{0,1},{1,2},{2,3},{3,4},{4,5},{5,6},{6,7},{7,8},{8,9},{9,10},{10,1... | collective-permute-start | bytes 393224 | tf_op jit(solution)/shard_map/ppermute | solution.py:21
  210.4 5.0 %collective-permute-start.11 = (f32[8,1,16,256]{3,2,1,0:T(8,128)S(1)}, f32[8,1,16,256]{3,2,1,0:T(8,128)S(1)}, u32[]{:S(2)}, u32[]{:S(2)}) collective-permute-start(f32[8,1,16,256]{3,2,1,0:T(8,128)S(1)} %get-tuple-element.106), channel_id=1, source_target_pairs={{1,0},{2,1},{3,2},{4,3},{5,4},{6,5},{7,6},{8,7},{9,8},{10,9},{11,1... | collective-permute-start | bytes 393224 | tf_op jit(solution)/shard_map/ppermute | solution.py:22
  210.7 9.9 %collective-permute-start.12 = (f32[8,1,16,256]{3,2,1,0:T(8,128)S(1)}, f32[8,1,16,256]{3,2,1,0:T(8,128)S(1)}, u32[]{:S(2)}, u32[]{:S(2)}) collective-permute-start(f32[8,1,16,256]{3,2,1,0:T(8,128)S(1)} %get-tuple-element.107), channel_id=1, source_target_pairs={{0,1},{1,2},{2,3},{3,4},{4,5},{5,6},{6,7},{7,8},{8,9},{9,10},{10,1... | collective-permute-start | bytes 393224 | tf_op jit(solution)/shard_map/ppermute | solution.py:21
  221.2 16.8 %collective-permute-start.13 = (f32[8,4,16,256]{3,2,1,0:T(8,128)S(1)}, f32[8,4,16,256]{3,2,1,0:T(8,128)S(1)}, u32[]{:S(2)}, u32[]{:S(2)}) collective-permute-start(f32[8,4,16,256]{3,2,1,0:T(8,128)S(1)} %fusion.24), channel_id=1, source_target_pairs={{0,64},{64,128},{128,192},{1,65},{65,129},{129,193},{2,66},{66,130... | collective-permute-start | bytes 1572872 | tf_op jit(solution)/shard_map/ppermute | solution.py:30
  238.6 4.0 collective-permute-start.14
  239.8 9.8 %collective-permute-start.15 = (f32[8,1,16,256]{3,2,1,0:T(8,128)S(1)}, f32[8,1,16,256]{3,2,1,0:T(8,128)S(1)}, u32[]{:S(2)}, u32[]{:S(2)}) collective-permute-start(f32[8,1,16,256]{3,2,1,0:T(8,128)S(1)} %get-tuple-element.97), channel_id=1, source_target_pairs={{0,1},{1,2},{2,3},{3,4},{4,5},{5,6},{6,7},{7,8},{8,9},{9,10},{10,1... | collective-permute-start | bytes 393224 | tf_op jit(solution)/shard_map/ppermute | solution.py:21
  250.3 15.9 %collective-permute-start.16 = (f32[8,4,16,256]{3,2,1,0:T(8,128)S(1)}, f32[8,4,16,256]{3,2,1,0:T(8,128)S(1)}, u32[]{:S(2)}, u32[]{:S(2)}) collective-permute-start(f32[8,4,16,256]{3,2,1,0:T(8,128)S(1)} %fusion.31), channel_id=1, source_target_pairs={{0,64},{64,128},{128,192},{1,65},{65,129},{129,193},{2,66},{66,130... | collective-permute-start | bytes 1572872 | tf_op jit(solution)/shard_map/ppermute | solution.py:30
  266.8 6.0 %collective-permute-start.17 = (f32[8,1,16,256]{3,2,1,0:T(8,128)S(1)}, f32[8,1,16,256]{3,2,1,0:T(8,128)S(1)}, u32[]{:S(2)}, u32[]{:S(2)}) collective-permute-start(f32[8,1,16,256]{3,2,1,0:T(8,128)S(1)} %get-tuple-element.86), channel_id=1, source_target_pairs={{1,0},{2,1},{3,2},{4,3},{5,4},{6,5},{7,6},{8,7},{9,8},{10,9},{11,1... | collective-permute-start | bytes 393224 | tf_op jit(solution)/shard_map/ppermute | solution.py:22
  268.1 9.8 %collective-permute-start.18 = (f32[8,1,16,256]{3,2,1,0:T(8,128)S(1)}, f32[8,1,16,256]{3,2,1,0:T(8,128)S(1)}, u32[]{:S(2)}, u32[]{:S(2)}) collective-permute-start(f32[8,1,16,256]{3,2,1,0:T(8,128)S(1)} %get-tuple-element.87), channel_id=1, source_target_pairs={{0,1},{1,2},{2,3},{3,4},{4,5},{5,6},{6,7},{7,8},{8,9},{9,10},{10,1... | collective-permute-start | bytes 393224 | tf_op jit(solution)/shard_map/ppermute | solution.py:21
  278.7 16.0 %collective-permute-start.19 = (f32[8,4,16,256]{3,2,1,0:T(8,128)S(1)}, f32[8,4,16,256]{3,2,1,0:T(8,128)S(1)}, u32[]{:S(2)}, u32[]{:S(2)}) collective-permute-start(f32[8,4,16,256]{3,2,1,0:T(8,128)S(1)} %fusion.38), channel_id=1, source_target_pairs={{0,64},{64,128},{128,192},{1,65},{65,129},{129,193},{2,66},{66,130... | collective-permute-start | bytes 1572872 | tf_op jit(solution)/shard_map/ppermute | solution.py:30
  295.2 11.0 %collective-permute-start.20 = (f32[8,1,16,256]{3,2,1,0:T(8,128)S(1)}, f32[8,1,16,256]{3,2,1,0:T(8,128)S(1)}, u32[]{:S(2)}, u32[]{:S(2)}) collective-permute-start(f32[8,1,16,256]{3,2,1,0:T(8,128)S(1)} %get-tuple-element.68), channel_id=1, source_target_pairs={{1,0},{2,1},{3,2},{4,3},{5,4},{6,5},{7,6},{8,7},{9,8},{10,9},{11,1... | collective-permute-start | bytes 393224 | tf_op jit(solution)/shard_map/ppermute | solution.py:22
  296.5 9.9 %collective-permute-start.21 = (f32[8,1,16,256]{3,2,1,0:T(8,128)S(1)}, f32[8,1,16,256]{3,2,1,0:T(8,128)S(1)}, u32[]{:S(2)}, u32[]{:S(2)}) collective-permute-start(f32[8,1,16,256]{3,2,1,0:T(8,128)S(1)} %get-tuple-element.69), channel_id=1, source_target_pairs={{0,1},{1,2},{2,3},{3,4},{4,5},{5,6},{6,7},{7,8},{8,9},{9,10},{10,1... | collective-permute-start | bytes 393224 | tf_op jit(solution)/shard_map/ppermute | solution.py:21
  307.5 3.9 collective-permute-start.22
  307.9 9.8 %collective-permute-start.23 = (f32[8,1,16,256]{3,2,1,0:T(8,128)S(1)}, f32[8,1,16,256]{3,2,1,0:T(8,128)S(1)}, u32[]{:S(2)}, u32[]{:S(2)}) collective-permute-start(f32[8,1,16,256]{3,2,1,0:T(8,128)S(1)} %get-tuple-element.67), channel_id=1, source_target_pairs={{0,1},{1,2},{2,3},{3,4},{4,5},{5,6},{6,7},{7,8},{8,9},{9,10},{10,1... | collective-permute-start | bytes 393224 | tf_op jit(solution)/shard_map/ppermute | solution.py:21
  318.4 17.5 %collective-permute-start.24 = (f32[8,4,16,256]{3,2,1,0:T(8,128)S(1)}, f32[8,4,16,256]{3,2,1,0:T(8,128)S(1)}, u32[]{:S(2)}, u32[]{:S(2)}) collective-permute-start(f32[8,4,16,256]{3,2,1,0:T(8,128)S(1)} %fusion.48), channel_id=1, source_target_pairs={{0,64},{64,128},{128,192},{1,65},{65,129},{129,193},{2,66},{66,130... | collective-permute-start | bytes 1572872 | tf_op jit(solution)/shard_map/ppermute | solution.py:30
  336.5 6.0 %collective-permute-start.25 = (f32[8,1,16,256]{3,2,1,0:T(8,128)S(1)}, f32[8,1,16,256]{3,2,1,0:T(8,128)S(1)}, u32[]{:S(2)}, u32[]{:S(2)}) collective-permute-start(f32[8,1,16,256]{3,2,1,0:T(8,128)S(1)} %get-tuple-element.56), channel_id=1, source_target_pairs={{1,0},{2,1},{3,2},{4,3},{5,4},{6,5},{7,6},{8,7},{9,8},{10,9},{11,1... | collective-permute-start | bytes 393224 | tf_op jit(solution)/shard_map/ppermute | solution.py:22
  337.5 9.8 %collective-permute-start.26 = (f32[8,1,16,256]{3,2,1,0:T(8,128)S(1)}, f32[8,1,16,256]{3,2,1,0:T(8,128)S(1)}, u32[]{:S(2)}, u32[]{:S(2)}) collective-permute-start(f32[8,1,16,256]{3,2,1,0:T(8,128)S(1)} %get-tuple-element.57), channel_id=1, source_target_pairs={{0,1},{1,2},{2,3},{3,4},{4,5},{5,6},{6,7},{7,8},{8,9},{9,10},{10,1... | collective-permute-start | bytes 393224 | tf_op jit(solution)/shard_map/ppermute | solution.py:21
  348.0 15.9 %collective-permute-start.27 = (f32[8,4,16,256]{3,2,1,0:T(8,128)S(1)}, f32[8,4,16,256]{3,2,1,0:T(8,128)S(1)}, u32[]{:S(2)}, u32[]{:S(2)}) collective-permute-start(f32[8,4,16,256]{3,2,1,0:T(8,128)S(1)} %get-tuple-element.6), channel_id=1, source_target_pairs={{0,64},{64,128},{128,192},{1,65},{65,129},{129,193},{2,66},{66,130... | collective-permute-start | bytes 1572872 | tf_op jit(solution)/shard_map/ppermute | solution.py:30
  364.5 7.6 %collective-permute-start.28 = (f32[8,1,16,256]{3,2,1,0:T(8,128)S(1)}, f32[8,1,16,256]{3,2,1,0:T(8,128)S(1)}, u32[]{:S(2)}, u32[]{:S(2)}) collective-permute-start(f32[8,1,16,256]{3,2,1,0:T(8,128)S(1)} %get-tuple-element.46), channel_id=1, source_target_pairs={{1,0},{2,1},{3,2},{4,3},{5,4},{6,5},{7,6},{8,7},{9,8},{10,9},{11,1... | collective-permute-start | bytes 393224 | tf_op jit(solution)/shard_map/ppermute | solution.py:22
  365.8 9.8 %collective-permute-start.29 = (f32[8,1,16,256]{3,2,1,0:T(8,128)S(1)}, f32[8,1,16,256]{3,2,1,0:T(8,128)S(1)}, u32[]{:S(2)}, u32[]{:S(2)}) collective-permute-start(f32[8,1,16,256]{3,2,1,0:T(8,128)S(1)} %get-tuple-element.47), channel_id=1, source_target_pairs={{0,1},{1,2},{2,3},{3,4},{4,5},{5,6},{6,7},{7,8},{8,9},{9,10},{10,1... | collective-permute-start | bytes 393224 | tf_op jit(solution)/shard_map/ppermute | solution.py:21
  376.2 15.9 %collective-permute-start.30 = (f32[8,4,16,256]{3,2,1,0:T(8,128)S(1)}, f32[8,4,16,256]{3,2,1,0:T(8,128)S(1)}, u32[]{:S(2)}, u32[]{:S(2)}) collective-permute-start(f32[8,4,16,256]{3,2,1,0:T(8,128)S(1)} %fusion.62), channel_id=1, source_target_pairs={{0,64},{64,128},{128,192},{1,65},{65,129},{129,193},{2,66},{66,130... | collective-permute-start | bytes 1572872 | tf_op jit(solution)/shard_map/ppermute | solution.py:30
  392.3 11.5 %copy-start = (f32[8,4,16,256]{3,2,1,0:T(8,128)}, f32[8,4,16,256]{3,2,1,0:T(8,128)S(1)}, u32[]{:S(2)}) copy-start(f32[8,4,16,256]{3,2,1,0:T(8,128)S(1)} %get-tuple-element.3) | copy-start | bytes 1572868
  392.7 8.0 %collective-permute-start.31 = (f32[8,1,16,256]{3,2,1,0:T(8,128)S(1)}, f32[8,1,16,256]{3,2,1,0:T(8,128)S(1)}, u32[]{:S(2)}, u32[]{:S(2)}) collective-permute-start(f32[8,1,16,256]{3,2,1,0:T(8,128)S(1)} %get-tuple-element.36), channel_id=1, source_target_pairs={{1,0},{2,1},{3,2},{4,3},{5,4},{6,5},{7,6},{8,7},{9,8},{10,9},{11,1... | collective-permute-start | bytes 393224 | tf_op jit(solution)/shard_map/ppermute | solution.py:22
  393.9 9.8 %collective-permute-start.32 = (f32[8,1,16,256]{3,2,1,0:T(8,128)S(1)}, f32[8,1,16,256]{3,2,1,0:T(8,128)S(1)}, u32[]{:S(2)}, u32[]{:S(2)}) collective-permute-start(f32[8,1,16,256]{3,2,1,0:T(8,128)S(1)} %get-tuple-element.37), channel_id=1, source_target_pairs={{0,1},{1,2},{2,3},{3,4},{4,5},{5,6},{6,7},{7,8},{8,9},{9,10},{10,1... | collective-permute-start | bytes 393224 | tf_op jit(solution)/shard_map/ppermute | solution.py:21
where the time goes:
time: 406 us; the launch traced here: 405 us
  starting transfers between devices  144 us (35%)
  waiting for transfers between devices  138 us (34%)
  local copies, waits for them, and re-layouts  106 us (26%)
  other arithmetic  15.4 us (4%)
    gather x2, local copies, waits for them, and re-layouts, coefficients(): stored = jnp.take(grain_energy, labels)  97.2 us
    ppermute x9, starting transfers between devices, from_behind(): return lax.ppermute(block, axis, route)  87.9 us
    ppermute x9, waiting for transfers between devices, from_behind(): return lax.ppermute(block, axis, route)  55.2 us
    ppermute x12, waiting for transfers between devices, padded_2(): before = lax.ppermute(last, axis, up)  53.8 us
    ppermute x12, waiting for transfers between devices, padded_2(): after = lax.ppermute(first, axis, down)  28.9 us
    ppermute x12, starting transfers between devices, padded_2(): before = lax.ppermute(last, axis, up)  28.3 us
    ppermute x12, starting transfers between devices, padded_2(): after = lax.ppermute(first, axis, down)  28.1 us
  transfers between devices with their start and end apart: 33, of which 31 were waited for; matrix products, arithmetic and copies ran while one was open for 25% of the time, Pallas kernels for 0%

commit v1 on v0

v1 whole, which is shorter than its diff:
```python
import functools
import math

import jax
import jax.numpy as jnp
from jax import lax
from jax.experimental import pallas as pl
from jax.experimental.pallas import tpu as pltpu
from jax.sharding import PartitionSpec as P

MESH = pl.DeviceIdType.MESH
ORDERS = 8
HALO = 6
ROWS = 4
EXT = ROWS + 2 * HALO
FINE_DT = 0.06
ROOT2 = math.sqrt(2.0)

NEEDED = {
    "u0": (1, 3, 4, 5),
    "u0p": (0, 2, 3, 4),
    "c1": (-1, -1, 3, 4),
    "c1p": (-1, -1, 2, 3),
    "a1": (-1, 1, 2, 3),
    "a1p": (-1, 0, 1, 2),
    "c2": (-1, -1, -1, 3),
    "c2p": (-1, -1, -1, 2),
    "b2": (-1, -1, 1, 2),
    "b2p": (-1, -1, 0, 1),
    "a2": (-1, -1, 0, 1),
    "b3": (-1, -1, -1, 1),
    "b3p": (-1, -1, -1, 0),
    "d3": (-1, -1, -1, 0),
}


def by_slice(tm, values):
    result = jnp.int32(values[0])
    for index in range(1, len(values)):
        result = jnp.where(tm >= index, jnp.int32(values[index]), result)
    return result


def exchange_kernel(lab_ref, msk_ref, lab_ext, msk_ext, local_sem, send_sem, recv_sem):
    tm, me = lax.axis_index("tm"), lax.axis_index("space")
    count = lax.axis_size("space")
    place = lax.rem(me, 4)

    def partner(distance):
        crossed = jnp.where(jnp.logical_or(place + distance < 0, place + distance > 3), 1, 0)
        half = lax.rem(tm // 2 + crossed, 2)
        return (half * 2 + lax.rem(tm, 2), lax.rem(me + distance + count, count))

    barrier = pltpu.get_barrier_semaphore()
    for distance in (-2, -1, 1, 2):
        pl.semaphore_signal(barrier, inc=1, device_id=partner(distance), device_id_type=MESH)
    own = [
        pltpu.make_async_copy(src, dst.at[pl.ds(HALO, ROWS)], local_sem.at[k])
        for k, (src, dst) in enumerate(((lab_ref, lab_ext), (msk_ref, msk_ext)))
    ]
    for copy in own:
        copy.start()
    pl.semaphore_wait(barrier, 4)
    moves = ((1, 0, 4, 2), (-1, 0, 4, 10), (2, 2, 2, 0), (-2, 0, 2, 14))
    copies = []
    for m, (distance, first, rows, there) in enumerate(moves):
        for k, (src, dst) in enumerate(((lab_ref, lab_ext), (msk_ref, msk_ext))):
            copies.append(
                pltpu.make_async_remote_copy(
                    src_ref=src.at[pl.ds(first, rows)],
                    dst_ref=dst.at[pl.ds(there, rows)],
                    send_sem=send_sem.at[2 * m + k],
                    recv_sem=recv_sem.at[2 * m + k],
                    device_id=partner(distance),
                    device_id_type=MESH,
                )
            )
    for copy in copies:
        copy.start()
    for copy in own:
        copy.wait()
    for copy in copies:
        copy.wait()


def exchange(labels, particles):
    shape = jax.ShapeDtypeStruct((EXT,) + labels.shape[1:], jnp.int32)
    return pl.pallas_call(
        exchange_kernel,
        out_shape=(shape, shape),
        in_specs=[pl.BlockSpec(memory_space=pl.ANY)] * 2,
        out_specs=[pl.BlockSpec(memory_space=pl.ANY)] * 2,
        scratch_shapes=[
            pltpu.SemaphoreType.DMA((2,)),
            pltpu.SemaphoreType.DMA((8,)),
            pltpu.SemaphoreType.DMA((8,)),
        ],
        compiler_params=pltpu.CompilerParams(collective_id=0, has_side_effects=True),
        name="exchange",
    )(labels, particles)


def lanes(shape=(8, 128)):
    return lax.broadcasted_iota(jnp.int32, shape, 1)


def pick(x, index):
    return jnp.take_along_axis(x, index, axis=1, mode="promise_in_bounds")


def apart(ref, row, zt, yt):
    low = ref[0, row, pl.ds(zt, 8, stride=2), :]
    high = ref[1, row, pl.ds(zt, 8, stride=2), :]
    index = lax.rem(2 * lanes() + yt, 128)
    return jnp.where(lanes() < 64, pick(low, index), pick(high, index))


def together(out, order, row, tiles):
    odd = lax.rem(lanes(), 2) == 1
    for zt in (0, 1):
        for half in (0, 1):
            index = lanes() // 2 + 64 * half
            mixed = jnp.where(odd, pick(tiles[2 * zt + 1], index), pick(tiles[2 * zt], index))
            out[half, order, row, pl.ds(zt, 8, stride=2), :] = mixed


def neighbours(ref, row, order):
    e = [ref[row, tile, order] for tile in range(4)]
    odd, even = e[1] + e[2], e[0] + e[3]
    beside = [
        odd + pltpu.roll(e[1], 1, 1) + pltpu.roll(e[2], 1, 0),
        even + pltpu.roll(e[0], 127, 1) + pltpu.roll(e[3], 1, 0),
        even + pltpu.roll(e[3], 1, 1) + pltpu.roll(e[0], 7, 0),
        odd + pltpu.roll(e[2], 127, 1) + pltpu.roll(e[1], 7, 0),
    ]
    total = [beside[tile] + (ref[row - 1, tile, order] + ref[row + 1, tile, order]) for tile in range(4)]
    return e, total


def annealing_kernel(
    lab_hbm, msk_hbm, class_ref, energy_ref, start_hbm, end_hbm,
    lab_ref, msk_ref, start_ref, end_ref, in_sem, out_sem, rate, drive, pinned, u0, u0p, c1, a1, c1p, c2, jump1, a1p, b2, c2p, jump2, b2p, b3, a2, jump3, d3, b3p, jump4, e4,
):
    tm = lax.axis_index("tm")

    copies = []
    for k, (src, dst) in enumerate(((lab_hbm, lab_ref), (msk_hbm, msk_ref))):
        for half in (0, 1):
            copies.append(pltpu.make_async_copy(src.at[:, :, pl.ds(128 * half, 128)], dst.at[half], in_sem.at[2 * k + half]))
    for copy in copies:
        copy.start()
    for copy in copies:
        copy.wait()

    classes = jnp.broadcast_to(class_ref[...], (8, 128))
    table = jnp.full((8, 128), energy_ref[0], jnp.float32)
    for kind in range(1, 4):
        table = jnp.where(classes == kind, energy_ref[kind], table)

    def prepare(row, carry):
        for tile in range(4):
            label = apart(lab_ref, row, tile // 2, tile % 2)
            particle = apart(msk_ref, row, tile // 2, tile % 2).astype(jnp.float32)
            rate[row, tile] = FINE_DT - (0.75 * FINE_DT) * particle
            stored = pick(table, label)
            center = (ROOT2 * 6.0) + ROOT2 * stored
            order = lax.rem(label, ORDERS)
            for p in range(ORDERS):
                mine = order == p
                u0[row, tile, p] = jnp.where(mine, ROOT2, 0.0)
                drive[row, tile, p] = jnp.where(mine, stored, 0.0)
                pinned[row, tile, p] = jnp.where(mine, center, 0.0)
        return carry

    lax.fori_loop(0, EXT, prepare, 0)

    def rows(name, body):
        reach = by_slice(tm, NEEDED[name])
        def once(row, carry):
            body(row)
            return carry
        lax.fori_loop(HALO - reach, jnp.where(reach < 0, HALO - reach, HALO + ROWS + reach), once, 0)

    def force(name, field, store):
        def body(row):
            squares = [[None] * ORDERS for _ in range(4)]
            level = []
            for tile in range(4):
                total = None
                for p in range(ORDERS):
                    center = field[row, tile, p]
                    squares[tile][p] = center * center
                    total = squares[tile][p] if total is None else total + squares[tile][p]
                level.append(1.5 * total + 5.0)
            speed = [rate[row, tile] for tile in range(4)]
            for p in range(ORDERS):
                e, beside = neighbours(field, row, p)
                for tile in range(4):
                    slope = squares[tile][p] - (level[tile] + drive[row, tile, p])
                    store(row, tile, p, e[tile], speed[tile] * (beside[tile] + e[tile] * slope))
        rows(name, body)

    def first(row):
        speed = [rate[row, tile] for tile in range(4)]
        for p in range(ORDERS):
            e, beside = neighbours(u0, row, p)
            for tile in range(4):
                change = speed[tile] * (beside[tile] - pinned[row, tile, p])
                half = e[tile] + change
                u0p[row, tile, p] = half
                c1[row, tile, p] = half + change

    rows("u0", first)

    def to_a1(row, tile, p, e, change):
        a1[row, tile, p] = e + change

    def to_c2(row, tile, p, e, change):
        half = e + change
        c1p[row, tile, p] = half
        c2[row, tile, p] = half + change
        jump1[row, tile, p] = change

    def to_jump1(row, tile, p, e, change):
        jump1[row, tile, p] = change - jump1[row, tile, p]

    def to_b2(row, tile, p, e, change):
        half = e + change
        a1p[row, tile, p] = half
        b2[row, tile, p] = half + (change + jump1[row, tile, p])

    def to_c2p(row, tile, p, e, change):
        c2p[row, tile, p] = e + change
        jump2[row, tile, p] = change

    def to_jump2(row, tile, p, e, change):
        jump2[row, tile, p] = change - jump2[row, tile, p]

    def to_b3(row, tile, p, e, change):
        half = e + change
        b2p[row, tile, p] = half
        b3[row, tile, p] = half + (change + jump2[row, tile, p])
        jump3[row, tile, p] = change

    def to_a2(row, tile, p, e, change):
        a2[row, tile, p] = e + change

    def to_jump3(row, tile, p, e, change):
        jump3[row, tile, p] = change - jump3[row, tile, p]

    def to_d3(row, tile, p, e, change):
        d3[row, tile, p] = (e + change) + (change + jump3[row, tile, p])

    def to_b3p(row, tile, p, e, change):
        b3p[row, tile, p] = e + change
        jump4[row, tile, p] = change

    def to_jump4(row, tile, p, e, change):
        jump4[row, tile, p] = change - jump4[row, tile, p]

    def to_e4(row, tile, p, e, change):
        e4[row, tile, p] = (e + change) + (change + jump4[row, tile, p])

    force("u0p", u0p, to_a1)
    force("c1", c1, to_c2)
    force("c1p", c1p, to_jump1)
    force("a1", a1, to_b2)
    force("a1p", a1p, to_a2)
    force("c2", c2, to_c2p)
    force("c2p", c2p, to_jump2)
    force("b2", b2, to_b3)
    force("b2p", b2p, to_jump3)
    force("a2", a2, to_d3)
    force("b3", b3, to_b3p)
    force("b3p", b3p, to_jump4)
    force("d3", d3, to_e4)

    def write(out, field):
        def once(row, carry):
            for p in range(ORDERS):
                tiles = [field[row + HALO, tile, p] * (1.0 / ROOT2) for tile in range(4)]
                together(out, p, row, tiles)
            return carry
        lax.fori_loop(0, ROWS, once, 0)

    results = (u0, a1, a2, d3, e4)
    for index in range(4):
        @pl.when(tm == index)
        def _():
            write(start_ref, results[index])
            write(end_ref, results[index + 1])

    copies = []
    for k, (src, dst) in enumerate(((start_ref, start_hbm), (end_ref, end_hbm))):
        for half in (0, 1):
            copies.append(pltpu.make_async_copy(src.at[half], dst.at[0, :, :, :, pl.ds(128 * half, 128)], out_sem.at[2 * k + half]))
    for copy in copies:
        copy.start()
    for copy in copies:
        copy.wait()


def annealing(lab_ext, msk_ext, grain_class, class_energy):
    out = jax.ShapeDtypeStruct((1, ORDERS, ROWS, 16, 256), jnp.float32)
    tiles = lambda *extra: pltpu.VMEM((EXT, 4) + extra + (8, 128), jnp.float32)
    return pl.pallas_call(
        annealing_kernel,
        out_shape=(out, out),
        in_specs=[pl.BlockSpec(memory_space=pl.ANY)] * 2
        + [pl.BlockSpec(memory_space=pltpu.VMEM), pl.BlockSpec(memory_space=pltpu.SMEM)],
        out_specs=[pl.BlockSpec(memory_space=pl.ANY)] * 2,
        scratch_shapes=[pltpu.VMEM((2, EXT, 16, 128), jnp.int32)] * 2
        + [pltpu.VMEM((2, ORDERS, ROWS, 16, 128), jnp.float32)] * 2
        + [pltpu.SemaphoreType.DMA((4,)), pltpu.SemaphoreType.DMA((4,))]
        + [tiles()]
        + [tiles(ORDERS)] * 21,
        compiler_params=pltpu.CompilerParams(vmem_limit_bytes=60 * 1024 * 1024),
        name="annealing",
    )(lab_ext, msk_ext, grain_class.reshape(1, -1), class_energy)


def local(grain_labels, particle_mask, grain_class, class_energy):
    lab_ext, msk_ext = exchange(grain_labels, particle_mask)
    return annealing(lab_ext, msk_ext, grain_class, class_energy)


def solution(mesh):
    placed = (P("space", None, None), P("space", None, None), P(), P())
    return jax.shard_map(
        local,
        mesh=mesh,
        in_specs=placed,
        out_specs=(P("tm", None, "space", None, None), P("tm", None, "space", None, None)),
        check_vma=False,
    )
```

time: 406 us -> 34.9 us (0.09)
  the two profiles are of different devices: /device:TPU:1 before, /device:TPU:255 now
where the time goes in v1:
time: 34.9 us; the launch traced here: 34.8 us
  Pallas kernels  34.2 us (98%)
  between operations  0.64 us (2%)
    pallas_call x1, Pallas kernels, annealing(): pl.pallas_call(annealing_kernel, out_shape=(out, out), in_specs=[pl.Block...  20.6 us
    pallas_call x1, Pallas kernels, exchange(): pl.pallas_call(exchange_kernel, out_shape=(shape, shape), in_specs=[pl.Bl...  13.6 us

profile of v1, /device:TPU:255, one launch (start us, length us, event | category | flops | bytes accessed | tf_op | source)
XLA Modules:
  0.0 34.8 jit_solution(18272639580151720777)
XLA Ops:
  0.6 13.6 %exchange.1 = (s32[16,16,256]{2,1,0:T(8,128)}, s32[16,16,256]{2,1,0:T(8,128)}) custom-call(s32[4,16,256]{2,1,0:T(8,128)} %lab_ref.1, s32[4,16,256]{2,1,0:T(8,128)} %msk_ref.1), custom_call_target="tpu_custom_call" | custom-call | tf_op jit(solution)/shard_map/exchange/pallas_call | solution.py:88
  14.2 20.6 %annealing.1 = (f32[1,8,4,16,256]{4,3,2,1,0:T(8,128)}, f32[1,8,4,16,256]{4,3,2,1,0:T(8,128)}) custom-call(s32[16,16,256]{2,1,0:T(8,128)} %get-tuple-element.4.lab_hbm, s32[16,16,256]{2,1,0:T(8,128)} %get-tuple-element.5.msk_hbm, s32[1,128]{1,0:T(1,128)} %bitcast.1, f32[4]{0:T(128)} %energy_ref.1), custom_call_target="tpu_custom_call" | custom-call | tf_op jit(solution)/shard_map/annealing/pallas_call | solution.py:306

commit v2 on v0

v2 whole, which is shorter than its diff:
```python
import functools
import math

import jax
import jax.numpy as jnp
from jax import lax
from jax.experimental import pallas as pl
from jax.experimental.pallas import tpu as pltpu
from jax.sharding import PartitionSpec as P

MESH = pl.DeviceIdType.MESH
ORDERS = 8
HALO = 6
ROWS = 4
EXT = ROWS + 2 * HALO
FINE_DT = 0.06
ROOT2 = math.sqrt(2.0)

REACH = {
    "1": (1, 3, 4, 5),
    "2": (0, 2, 3, 4),
    "3": (-1, 1, 2, 3),
    "4": (-1, 0, 1, 2),
    "5": (-1, -1, 0, 1),
    "6": (-1, -1, -1, 0),
}


def by_slice(tm, values):
    result = jnp.int32(values[0])
    for index in range(1, len(values)):
        result = jnp.where(tm >= index, jnp.int32(values[index]), result)
    return result


TURN = (1, 127)


def order_of_lanes(across):
    y = lax.broadcasted_iota(jnp.int32, (256, 256), across)
    place = lax.broadcasted_iota(jnp.int32, (256, 256), 1 - across)
    return jnp.where(y == 2 * (place & 127) + (place >> 7), 1.0, 0.0).astype(jnp.bfloat16)


class View:
    def __init__(self, store, first, orders):
        self.store, self.first, self.orders = store, first, orders

    def at(self, index):
        return (index[0], self.first + index[1] * self.orders + (index[2] if self.orders > 1 else 0))

    def __getitem__(self, index):
        return self.store[self.at(index)]

    def __setitem__(self, index, tile):
        self.store[self.at(index)] = tile

    def brick(self, tile):
        return self.store[pl.ds(HALO, ROWS), pl.ds(self.first + tile * self.orders, self.orders)]


class Shelf:
    def __init__(self, store):
        self.store, self.used = store, 0

    def planes(self):
        return self.view(1)

    def field(self):
        return self.view(ORDERS)

    def view(self, orders):
        self.used += 4 * orders
        return View(self.store, self.used - 4 * orders, orders)


FIXED = 4 * (3 + ORDERS)
PLACES = 4 * (ORDERS + 3 * (3 * ORDERS + 1))


class Field:
    def __init__(self, shelf):
        self.value, self.turned, self.term, self.level = shelf.field(), shelf.field(), shelf.field(), shelf.planes()


def around(field, row, tile, order):
    e, beyond = field.value[row, tile, order], field.value[row, tile ^ 2, order]
    along_y = field.value[row, tile ^ 1, order] + field.turned[row, tile, order]
    along_z = beyond + pltpu.roll(beyond, 1 if tile < 2 else 7, 0)
    return e, (along_y + along_z) + (field.value[row - 1, tile, order] + field.value[row + 1, tile, order])


MOVES = (
    (1, 1, 0, 2, 6, 4, 2),
    (-1, 1, 0, 2, 6, 4, 10),
    (2, 3, 0, 1, 8, 2, 0),
    (-2, 3, 0, 1, 6, 2, 14),
    (2, 3, 1, 1, 9, 1, 1),
    (-2, 3, 1, 1, 6, 1, 14),
)
HANDED = ((1, 4, 2, 6), (1, 10, 2, 7), (3, 2, 4, 6), (3, 10, 4, 7), (3, 1, 1, 8), (3, 14, 1, 9))


def annealing_kernel(
    lab_hbm, msk_hbm, class_hbm, energy_hbm, start_hbm, end_hbm,
    cells, class_ref, energy_ref, result, in_sem, send_sem, recv_sem, out_sem, deal, gather, code, marks, fixed, store_a, store_b,
):
    tm, me = lax.axis_index("tm"), lax.axis_index("space")
    count = lax.axis_size("space")
    place = lax.rem(me, 4)

    local_copies = [
        pltpu.make_async_copy(
            src.at[:, :, pl.ds(128 * half, 128)], cells.at[k, half, pl.ds(HALO, ROWS)], in_sem.at[2 * k + half]
        )
        for k, src in enumerate((lab_hbm, msk_hbm))
        for half in (0, 1)
    ]
    table_copies = [
        pltpu.make_async_copy(class_hbm, class_ref, in_sem.at[4]),
        pltpu.make_async_copy(energy_hbm, energy_ref, in_sem.at[5]),
    ]
    for copy in local_copies + table_copies:
        copy.start()

    def partner(distance):
        crossed = jnp.where(jnp.logical_or(place + distance < 0, place + distance > 3), 1, 0)
        half = lax.rem(tm // 2 + crossed, 2)
        return half * 2 + lax.rem(tm, 2), lax.rem(me + distance + count, count)

    odd = lax.rem(tm, 2) == 1

    def greet(device):
        pl.semaphore_signal(barrier, inc=1, device_id=device, device_id_type=MESH)

    barrier = pltpu.get_barrier_semaphore()

    @pl.when(odd)
    def _():
        for distance in (1, -1):
            greet(partner(distance))

    @pl.when(tm == 3)
    def _():
        for distance in (2, -2):
            greet(partner(distance))

    @pl.when(jnp.logical_not(odd))
    def _():
        greet((tm + 1, me))

    far = [partner(distance)[0] == 3 for distance in (2, -2)]

    def halo(moves, sending, act):
        for m in moves:
            distance, least, array, arrays, first, rows, there = MOVES[m]
            target = partner(distance)
            copy = pltpu.make_async_remote_copy(
                src_ref=cells.at[pl.ds(array, arrays), :, pl.ds(first, rows)],
                dst_ref=cells.at[pl.ds(array, arrays), :, pl.ds(there, rows)],
                send_sem=send_sem.at[m],
                recv_sem=recv_sem.at[m],
                device_id=target,
                device_id_type=MESH,
            )
            receiver = target[0] if sending else tm
            wanted = jnp.logical_and(odd, receiver >= least)
            pl.when(wanted)(functools.partial(act, copy))

    def hand(copies, sending, act):
        for h in copies:
            holder, first, rows, sem = HANDED[h]
            copy = pltpu.make_async_remote_copy(
                src_ref=cells.at[:, :, pl.ds(first, rows)],
                dst_ref=cells.at[:, :, pl.ds(first, rows)],
                send_sem=send_sem.at[sem],
                recv_sem=recv_sem.at[sem],
                device_id=(holder - 1, me),
                device_id_type=MESH,
            )
            pl.when(tm == (holder if sending else holder - 1))(functools.partial(act, copy))

    start, sent, received = (lambda copy: copy.start()), (lambda copy: copy.wait_send()), (lambda copy: copy.wait_recv())

    for row in (0, EXT - 1):
        for half in (0, 1):
            cells[1, half, row] = jnp.zeros((16, 128), jnp.int32)
    for copy in local_copies:
        copy.wait()

    @pl.when(odd)
    def _():
        pl.semaphore_wait(barrier, 3 + jnp.where(far[0], 1, 0) + jnp.where(far[1], 1, 0))

    halo(range(6), True, start)

    for copy in table_copies:
        copy.wait()
    deal[...] = order_of_lanes(0)
    gather[...] = order_of_lanes(1)
    classes = jnp.broadcast_to(class_ref[...], (8, 128))
    table = jnp.full((8, 128), energy_ref[0], jnp.float32)
    for kind in range(1, 4):
        table = jnp.where(classes == kind, energy_ref[kind], table)

    shelf = Shelf(fixed)
    rate, base, weight, drive = shelf.planes(), shelf.planes(), shelf.planes(), shelf.field()
    shelf = Shelf(store_a)
    held_a, (a1, c1p, c2) = shelf.field(), [Field(shelf) for _ in range(3)]
    shelf = Shelf(store_b)
    held_b, (a1p, b2, c2p) = shelf.field(), [Field(shelf) for _ in range(3)]
    a2, b2p, b3 = a1, c1p, c2
    u0p, c1 = d3, b3p = a1p, b2

    def unpack(first, rows):
        for zt in (0, 1):
            found = None
            for half in (0, 1):
                there = (pl.ds(first, rows), pl.ds(zt, 8, stride=2))
                both = cells[0, half, *there] + 128 * cells[1, half, *there]
                part = jnp.dot(
                    both.astype(jnp.float32).reshape(rows * 8, 128).astype(jnp.bfloat16),
                    deal[pl.ds(128 * half, 128), :],
                    preferred_element_type=jnp.float32,
                )
                found = part if found is None else found + part
            found = found.astype(jnp.int32).reshape(rows, 8, 256)
            for yt in (0, 1):
                code[pl.ds(first, rows), 2 * zt + yt] = found[:, :, 128 * yt : 128 * yt + 128]

    def prepare(row):
        for tile in range(4):
            both = code[row, tile]
            label = both & 127
            rate[row, tile] = jnp.where(both > 127, 0.25 * FINE_DT, FINE_DT)
            stored = jnp.take_along_axis(table, label, axis=1, mode="promise_in_bounds")
            base[row, tile] = 1.5 * stored + 5.0
            weight[row, tile] = ROOT2 * stored + ROOT2 * 6.0
            order = both & (ORDERS - 1)
            mark = jnp.left_shift(1, 4 * order)
            marks[row, tile] = mark
            marks[row, 4 + (tile ^ 1)] = pltpu.roll(mark, TURN[1 - (tile & 1)], 1)
            for p in range(ORDERS):
                drive[row, tile, p] = jnp.where(order == p, stored, 0.0)

    def pairs(first, count, body):
        def once(k, carry):
            body(first + 2 * k)
            body(first + 2 * k + 1)
            return carry
        lax.fori_loop(0, count, once, 0)

    def level_of(name, body):
        reach = by_slice(tm, REACH[name])
        pairs(HALO - reach, jnp.where(reach < 0, 0, ROWS // 2 + reach), body)

    class Made:
        def __init__(self, field, row):
            self.field, self.row, self.total = field, row, [None] * 4

        def __call__(self, tile, p, value):
            self.field.value[self.row, tile, p] = value
            self.field.turned[self.row, tile ^ 1, p] = pltpu.roll(value, TURN[1 - (tile & 1)], 1)
            part = value * value - drive[self.row, tile, p]
            self.field.term[self.row, tile, p] = part
            self.total[tile] = part if p == 0 else self.total[tile] + part
            if p == ORDERS - 1:
                self.field.level[self.row, tile] = 1.5 * self.total[tile] + base[self.row, tile]

    def force(field, row, tile, p):
        e, beside = around(field, row, tile, p)
        return e, beside + e * (field.term[row, tile, p] - field.level[row, tile])

    def changed(field, row, tile, p, speed):
        e, push = force(field, row, tile, p)
        return e, speed * push

    even = lax.rem(lax.broadcasted_iota(jnp.int32, (8, 128), 1), 2) == 0
    spread = [lax.broadcasted_iota(jnp.int32, (8, 128), 1) // 2 + 64 * half for half in (0, 1)]

    def together(which, row, p, zt, tiles):
        for half in (0, 1):
            left, right = (jnp.take_along_axis(t, spread[half], axis=1, mode="promise_in_bounds") for t in tiles)
            result[which, half, p, row - HALO + 1, pl.ds(zt, 8, stride=2), :] = jnp.where(even, left, right) * (1.0 / ROOT2)

    def level1(row):
        new_u0p, new_c1 = Made(u0p, row), Made(c1, row)
        for tile in range(4):
            beyond = marks[row, tile ^ 2]
            beside = marks[row, tile ^ 1] + marks[row, 4 + tile] + beyond + pltpu.roll(beyond, 1 if tile < 2 else 7, 0)
            beside = beside + marks[row - 1, tile] + marks[row + 1, tile]
            order = code[row, tile] & (ORDERS - 1)
            speed = rate[row, tile]
            quick, own = ROOT2 * speed, ROOT2 - speed * weight[row, tile]
            for p in range(ORDERS):
                mine = order == p
                share = quick * (jnp.right_shift(beside, 4 * p) & 7).astype(jnp.float32)
                half = share + jnp.where(mine, own, 0.0)
                new_u0p(tile, p, half)
                new_c1(tile, p, (half + half) - jnp.where(mine, ROOT2, 0.0))

    def level2(row):
        new_a1, new_c1p, new_c2 = Made(a1, row), Made(c1p, row), Made(c2, row)
        for tile in range(4):
            speed = rate[row, tile]
            for p in range(ORDERS):
                e, change = changed(u0p, row, tile, p, speed)
                new_a1(tile, p, e + change)
            for p in range(ORDERS):
                e, change = changed(c1, row, tile, p, speed)
                half = e + change
                new_c1p(tile, p, half)
                new_c2(tile, p, half + change)
                held_a[row, tile, p] = change

    def level3(row):
        new_a1p, new_b2, new_c2p = Made(a1p, row), Made(b2, row), Made(c2p, row)
        for tile in range(4):
            speed = rate[row, tile]
            for p in range(ORDERS):
                jump = changed(c1p, row, tile, p, speed)[1] - held_a[row, tile, p]
                e, change = changed(a1, row, tile, p, speed)
                half = e + change
                new_a1p(tile, p, half)
                new_b2(tile, p, half + (change + jump))
            for p in range(ORDERS):
                e, change = changed(c2, row, tile, p, speed)
                new_c2p(tile, p, e + change)
                held_b[row, tile, p] = change

    def level4(row):
        new_a2, new_b2p, new_b3 = Made(a2, row), Made(b2p, row), Made(b3, row)
        for tile in range(4):
            speed = rate[row, tile]
            for p in range(ORDERS):
                e, change = changed(a1p, row, tile, p, speed)
                new_a2(tile, p, e + change)
            for p in range(ORDERS):
                jump = changed(c2p, row, tile, p, speed)[1] - held_b[row, tile, p]
                e, push = force(b2, row, tile, p)
                change = speed * push
                half = e + change
                new_b2p(tile, p, half)
                new_b3(tile, p, half + (change + jump))
                held_a[row, tile, p] = push

    def level5(row):
        which = jnp.where(tm == 2, 1, 0)
        new_d3, new_b3p = Made(d3, row), Made(b3p, row)
        for zt in (0, 1):
            for p in range(ORDERS):
                tiles = []
                for tile in (2 * zt, 2 * zt + 1):
                    jump = force(b2p, row, tile, p)[1] - held_a[row, tile, p]
                    e, push = force(a2, row, tile, p)
                    tiles.append(e + rate[row, tile] * (push + (push + jump)))
                    new_d3(tile, p, tiles[-1])
                together(which, row, p, zt, tiles)
        for tile in range(4):
            speed = rate[row, tile]
            for p in range(ORDERS):
                e, push = force(b3, row, tile, p)
                new_b3p(tile, p, e + speed * push)
                held_b[row, tile, p] = push

    def level6(row):
        for zt in (0, 1):
            for p in range(ORDERS):
                tiles = []
                for tile in (2 * zt, 2 * zt + 1):
                    jump = force(b3p, row, tile, p)[1] - held_b[row, tile, p]
                    e, push = force(d3, row, tile, p)
                    tiles.append(e + rate[row, tile] * (push + (push + jump)))
                together(1, row, p, zt, tiles)

    outs = (start_hbm, end_hbm)

    def sends(which):
        return [
            pltpu.make_async_copy(
                result.at[which, half, :, pl.ds(1, ROWS)],
                outs[which].at[0, :, :, :, pl.ds(128 * half, 128)],
                out_sem.at[2 * which + half],
            )
            for half in (0, 1)
        ]

    def send(ends, starts):
        for which, holder in enumerate((starts, ends)):
            @pl.when(tm == holder)
            def _():
                for copy in sends(which):
                    copy.start()

    def write(field, ends, starts):
        @pl.when(jnp.logical_or(tm == ends, tm == starts))
        def _():
            which = jnp.where(tm == ends, 1, 0)
            for zt in (0, 1):
                pieces = []
                for yt in (0, 1):
                    rest = field.value.brick(2 * zt + yt).reshape(ROWS * ORDERS * 8, 128) * (1.0 / ROOT2)
                    parts = []
                    for _ in range(3):
                        parts.append(rest.astype(jnp.bfloat16))
                        rest = rest - parts[-1].astype(jnp.float32)
                    pieces.append(parts)
                mixed = None
                for left, right in zip(*pieces):
                    moved = jnp.dot(jnp.concatenate([left, right], axis=1), gather[...], preferred_element_type=jnp.float32)
                    mixed = moved if mixed is None else mixed + moved
                mixed = mixed.reshape(ROWS, ORDERS, 8, 256)
                for row in range(ROWS):
                    for half in (0, 1):
                        result[which, half, :, row + 1, pl.ds(zt, 8, stride=2), :] = mixed[row, :, :, 128 * half : 128 * half + 128]

        send(ends, starts)

    @pl.when(tm == 0)
    def _():
        for half in (0, 1):
            for row in range(ROWS):
                order = cells[0, half, HALO + row] & (ORDERS - 1)
                for p in range(ORDERS):
                    result[0, half, p, row + 1] = jnp.where(order == p, 1.0, 0.0)

    send(-1, 0)
    unpack(HALO, ROWS)
    pairs(HALO, ROWS // 2, prepare)
    halo((0, 1), False, received)
    hand((0, 1, 2, 3), True, start)
    hand((0, 1, 2, 3), False, received)
    for first in (HALO - 4, HALO + ROWS):
        unpack(first, 4)
        pairs(first, 2, prepare)
    reach = by_slice(tm, REACH["1"])
    nearer = jnp.minimum(reach, 3)
    pairs(HALO - nearer, ROWS // 2 + nearer, level1)
    halo((2, 3, 4, 5), False, received)
    hand((4, 5), True, start)
    hand((4, 5), False, received)

    @pl.when(reach > 3)
    def _():
        for first in (0, EXT - 2):
            unpack(first, 2)
        pairs(0, 2, lambda row: prepare(jnp.where(row >= 2, row + EXT - 4, row)))
        pairs(0, 2, lambda row: level1(jnp.where(row >= 2, row + EXT - 5, row + 1)))

    level_of("2", level2)
    write(a1, 0, 1)
    level_of("3", level3)
    level_of("4", level4)
    write(a2, 1, 2)
    level_of("5", level5)
    send(2, 3)
    level_of("6", level6)
    send(3, -1)
    halo(range(6), True, sent)
    hand(range(6), True, sent)
    for which in (0, 1):
        for copy in sends(which):
            copy.wait()


def annealing(labels, particles, grain_class, class_energy):
    out = jax.ShapeDtypeStruct((1, ORDERS, ROWS, 16, 256), jnp.float32)
    arguments = [labels, particles, grain_class.reshape(1, -1), class_energy]
    return pl.pallas_call(
        annealing_kernel,
        out_shape=(out, out),
        in_specs=[pl.BlockSpec(memory_space=pltpu.HBM)] * 4,
        out_specs=[pl.BlockSpec(memory_space=pl.ANY)] * 2,
        scratch_shapes=[
            pltpu.VMEM((2, 2, EXT, 16, 128), jnp.int32),
            pltpu.VMEM((1, 128), jnp.int32),
            pltpu.SMEM((4,), jnp.float32),
            pltpu.VMEM((2, 2, ORDERS, ROWS + 2, 16, 128), jnp.float32),
            pltpu.SemaphoreType.DMA((6,)),
            pltpu.SemaphoreType.DMA((10,)),
            pltpu.SemaphoreType.DMA((10,)),
            pltpu.SemaphoreType.DMA((4,)),
            pltpu.VMEM((256, 256), jnp.bfloat16),
            pltpu.VMEM((256, 256), jnp.bfloat16),
            pltpu.VMEM((EXT, 4, 8, 128), jnp.int32),
            pltpu.VMEM((EXT, 8, 8, 128), jnp.int32),
        ]
        + [pltpu.VMEM((EXT, places, 8, 128), jnp.float32) for places in (FIXED, PLACES, PLACES)],
        compiler_params=pltpu.CompilerParams(
            collective_id=0, has_side_effects=True, vmem_limit_bytes=52 * 1024 * 1024
        ),
        name="annealing",
    )(*(pltpu.with_memory_space_constraint(a, pltpu.HBM) for a in arguments))


def solution(mesh):
    placed = (P("space", None, None), P("space", None, None), P(), P())
    return jax.shard_map(
        annealing,
        mesh=mesh,
        in_specs=placed,
        out_specs=(P("tm", None, "space", None, None), P("tm", None, "space", None, None)),
        check_vma=False,
    )
```

time: 406 us -> 24.3 us (0.06)
  the two profiles are of different devices: /device:TPU:1 before, /device:TPU:255 now
where the time goes in v2:
time: 24.3 us; the launch traced here: 24.1 us
  Pallas kernels  21.9 us (90%)
  local copies, waits for them, and re-layouts  1.59 us (7%)
  between operations  0.64 us (3%)
    pallas_call x1, Pallas kernels, annealing(): pl.pallas_call(annealing_kernel, out_shape=(out, out), in_specs=[pl.Block...  21.9 us
    unnamed x2, local copies, waits for them, and re-layouts  1.59 us

profile of v2, /device:TPU:255, one launch (start us, length us, event | category | flops | bytes accessed | tf_op | source)
XLA Modules:
  0.0 24.1 jit_solution(1388757499969633336)
XLA Ops:
  0.6 21.9 %annealing.1 = (f32[1,8,4,16,256]{4,3,2,1,0:T(8,128)S(1)}, f32[1,8,4,16,256]{4,3,2,1,0:T(8,128)S(1)}) custom-call(s32[4,16,256]{2,1,0:T(8,128)} %lab_hbm.1, s32[4,16,256]{2,1,0:T(8,128)} %msk_hbm.1, s32[1,128]{1,0:T(1,128)} %bitcast.1, f32[4]{0:T(128)} %energy_hbm.1), custom_call_target="tpu_custom_call" | custom-call | tf_op jit(solution)/shard_map/annealing/pallas_call | solution.py:469
  22.5 0.8 %copy.8 = f32[1,8,4,16,256]{4,3,2,1,0:T(8,128)} copy(f32[1,8,4,16,256]{4,3,2,1,0:T(8,128)S(1)} %get-tuple-element.4) | data formatting | bytes 1048576
  23.3 0.8 %copy.9 = f32[1,8,4,16,256]{4,3,2,1,0:T(8,128)} copy(f32[1,8,4,16,256]{4,3,2,1,0:T(8,128)S(1)} %get-tuple-element.5) | data formatting | bytes 1048576

commit v3 on v2

--- a/solution.py
+++ b/solution.py
@@ -99,6 +99,9 @@
     (-2, 3, 1, 1, 6, 1, 14),
 )
 HANDED = ((1, 4, 2, 6), (1, 10, 2, 7), (3, 2, 4, 6), (3, 10, 4, 7), (3, 1, 1, 8), (3, 14, 1, 9))
+
+
+SIDES = (((0,), (2, 4), (0, 2), (4,)), ((1,), (3, 5), (1, 3), (5,)))
 
 
 def annealing_kernel(
@@ -210,6 +213,7 @@
     shelf = Shelf(store_b)
     held_b, (a1p, b2, c2p) = shelf.field(), [Field(shelf) for _ in range(3)]
     a2, b2p, b3 = a1, c1p, c2
+    e4 = a1
     u0p, c1 = d3, b3p = a1p, b2
 
     def unpack(first, rows):
@@ -275,20 +279,10 @@
         e, push = force(field, row, tile, p)
         return e, speed * push
 
-    even = lax.rem(lax.broadcasted_iota(jnp.int32, (8, 128), 1), 2) == 0
-    spread = [lax.broadcasted_iota(jnp.int32, (8, 128), 1) // 2 + 64 * half for half in (0, 1)]
-
-    def together(which, row, p, zt, tiles):
-        for half in (0, 1):
-            left, right = (jnp.take_along_axis(t, spread[half], axis=1, mode="promise_in_bounds") for t in tiles)
-            result[which, half, p, row - HALO + 1, pl.ds(zt, 8, stride=2), :] = jnp.where(even, left, right) * (1.0 / ROOT2)
-
     def level1(row):
         new_u0p, new_c1 = Made(u0p, row), Made(c1, row)
         for tile in range(4):
-            beyond = marks[row, tile ^ 2]
-            beside = marks[row, tile ^ 1] + marks[row, 4 + tile] + beyond + pltpu.roll(beyond, 1 if tile < 2 else 7, 0)
-            beside = beside + marks[row - 1, tile] + marks[row + 1, tile]
+            beside = counts(row, tile)
             order = code[row, tile] & (ORDERS - 1)
             speed = rate[row, tile]
             quick, own = ROOT2 * speed, ROOT2 - speed * weight[row, tile]
@@ -345,33 +339,56 @@
                 held_a[row, tile, p] = push
 
     def level5(row):
-        which = jnp.where(tm == 2, 1, 0)
         new_d3, new_b3p = Made(d3, row), Made(b3p, row)
-        for zt in (0, 1):
-            for p in range(ORDERS):
-                tiles = []
-                for tile in (2 * zt, 2 * zt + 1):
-                    jump = force(b2p, row, tile, p)[1] - held_a[row, tile, p]
-                    e, push = force(a2, row, tile, p)
-                    tiles.append(e + rate[row, tile] * (push + (push + jump)))
-                    new_d3(tile, p, tiles[-1])
-                together(which, row, p, zt, tiles)
-        for tile in range(4):
-            speed = rate[row, tile]
+        for tile in range(4):
+            speed = rate[row, tile]
+            for p in range(ORDERS):
+                jump = force(b2p, row, tile, p)[1] - held_a[row, tile, p]
+                e, push = force(a2, row, tile, p)
+                new_d3(tile, p, e + speed * (push + (push + jump)))
             for p in range(ORDERS):
                 e, push = force(b3, row, tile, p)
                 new_b3p(tile, p, e + speed * push)
                 held_b[row, tile, p] = push
 
     def level6(row):
-        for zt in (0, 1):
-            for p in range(ORDERS):
-                tiles = []
-                for tile in (2 * zt, 2 * zt + 1):
-                    jump = force(b3p, row, tile, p)[1] - held_b[row, tile, p]
-                    e, push = force(d3, row, tile, p)
-                    tiles.append(e + rate[row, tile] * (push + (push + jump)))
-                together(1, row, p, zt, tiles)
+        for tile in range(4):
+            speed = rate[row, tile]
+            for p in range(ORDERS):
+                jump = force(b3p, row, tile, p)[1] - held_b[row, tile, p]
+                e, push = force(d3, row, tile, p)
+                e4.value[row, tile, p] = e + speed * (push + (push + jump))
+
+    def counts(row, tile):
+        beyond = marks[row, tile ^ 2]
+        beside = marks[row, tile ^ 1] + marks[row, 4 + tile] + beyond + pltpu.roll(beyond, 1 if tile < 2 else 7, 0)
+        return beside + marks[row - 1, tile] + marks[row + 1, tile]
+
+    def short1(row):
+        new_u0p = Made(u0p, row)
+        for tile in range(4):
+            beside, order, speed = counts(row, tile), code[row, tile] & (ORDERS - 1), rate[row, tile]
+            quick, own = ROOT2 * speed, ROOT2 - speed * weight[row, tile]
+            for p in range(ORDERS):
+                share = quick * (jnp.right_shift(beside, 4 * p) & 7).astype(jnp.float32)
+                new_u0p(tile, p, share + jnp.where(order == p, own, 0.0))
+
+    def short(field, made):
+        def body(row):
+            new = Made(made, row)
+            for tile in range(4):
+                speed = rate[row, tile]
+                for p in range(ORDERS):
+                    e, change = changed(field, row, tile, p, speed)
+                    new(tile, p, e + change)
+        return body
+
+    def short4(row):
+        for tile in range(4):
+            speed = rate[row, tile]
+            for p in range(ORDERS):
+                e, change = changed(a1p, row, tile, p, speed)
+                a2.value[row, tile, p] = e + change
 
     outs = (start_hbm, end_hbm)
 
@@ -399,9 +416,9 @@
             for zt in (0, 1):
                 pieces = []
                 for yt in (0, 1):
-                    rest = field.value.brick(2 * zt + yt).reshape(ROWS * ORDERS * 8, 128) * (1.0 / ROOT2)
+                    rest = field.value.brick(2 * zt + yt).reshape(ROWS * ORDERS * 8, 128)
                     parts = []
-                    for _ in range(3):
+                    for _ in range(2):
                         parts.append(rest.astype(jnp.bfloat16))
                         rest = rest - parts[-1].astype(jnp.float32)
                     pieces.append(parts)
@@ -422,40 +439,72 @@
             for row in range(ROWS):
                 order = cells[0, half, HALO + row] & (ORDERS - 1)
                 for p in range(ORDERS):
-                    result[0, half, p, row + 1] = jnp.where(order == p, 1.0, 0.0)
+                    result[0, half, p, row + 1] = jnp.where(order == p, ROOT2, 0.0)
 
     send(-1, 0)
     unpack(HALO, ROWS)
     pairs(HALO, ROWS // 2, prepare)
-    halo((0, 1), False, received)
-    hand((0, 1, 2, 3), True, start)
-    hand((0, 1, 2, 3), False, received)
-    for first in (HALO - 4, HALO + ROWS):
+
+    low_late = jnp.logical_or(place < 2, me == 2)
+
+    def split(level, phase, lo, hi):
+        reach = by_slice(tm, REACH[level])
+        total = jnp.where(reach < 0, 0, ROWS // 2 + reach)
+        depth = int(level)
+        low = jnp.minimum((depth + reach + 1) // 2, total)
+        high = total - jnp.maximum((ROWS - depth + reach) // 2, 0)
+        late = jnp.where(low_late, low, high)
+        late = jnp.clip(late, 0, total)
+        number = jnp.where(phase == 0, total - late, late)
+        at_low = jnp.logical_xor(low_late, phase == 0)
+        first = HALO - reach + jnp.where(at_low, 0, 2 * (total - number))
+        return first, jnp.where(jnp.logical_and(tm >= lo, tm <= hi), number, 0)
+
+    def phases(phase, carry):
+        at_low = jnp.logical_xor(low_late, phase == 0)
+        for side, (halos, far_halos, hands, far_hands) in enumerate(SIDES):
+            @pl.when(at_low if side == 0 else jnp.logical_not(at_low))
+            def _():
+                halo(halos, False, received)
+                hand(hands, True, start)
+                hand(hands, False, received)
+        first = jnp.where(at_low, HALO - 4, HALO + ROWS)
         unpack(first, 4)
         pairs(first, 2, prepare)
-    reach = by_slice(tm, REACH["1"])
-    nearer = jnp.minimum(reach, 3)
-    pairs(HALO - nearer, ROWS // 2 + nearer, level1)
-    halo((2, 3, 4, 5), False, received)
-    hand((4, 5), True, start)
-    hand((4, 5), False, received)
-
-    @pl.when(reach > 3)
-    def _():
-        for first in (0, EXT - 2):
-            unpack(first, 2)
-        pairs(0, 2, lambda row: prepare(jnp.where(row >= 2, row + EXT - 4, row)))
-        pairs(0, 2, lambda row: level1(jnp.where(row >= 2, row + EXT - 5, row + 1)))
-
-    level_of("2", level2)
-    write(a1, 0, 1)
-    level_of("3", level3)
-    level_of("4", level4)
+        for side, (halos, far_halos, hands, far_hands) in enumerate(SIDES):
+            @pl.when(at_low if side == 0 else jnp.logical_not(at_low))
+            def _():
+                halo(far_halos, False, received)
+                hand(far_hands, True, start)
+                hand(far_hands, False, received)
+
+        @pl.when(tm >= 2)
+        def _():
+            outer = jnp.where(at_low, 0, EXT - 2)
+            unpack(outer, 2)
+            pairs(outer, 1, prepare)
+
+        pairs(*split("1", phase, 2, 3), level1)
+        pairs(*split("1", phase, 0, 1), short1)
+        pairs(*split("2", phase, 2, 3), level2)
+        pairs(*split("2", phase, 0, 1), short(u0p, a1))
+
+        @pl.when(phase == 1)
+        def _():
+            write(a1, 0, 1)
+
+        pairs(*split("3", phase, 2, 3), level3)
+        pairs(*split("3", phase, 0, 1), short(a1, a1p))
+        pairs(*split("4", phase, 2, 3), level4)
+        pairs(*split("4", phase, 0, 1), short4)
+        return carry
+
+    lax.fori_loop(0, 2, phases, 0)
     write(a2, 1, 2)
     level_of("5", level5)
-    send(2, 3)
+    write(d3, 2, 3)
     level_of("6", level6)
-    send(3, -1)
+    write(e4, 3, -1)
     halo(range(6), True, sent)
     hand(range(6), True, sent)
     for which in (0, 1):
@@ -466,7 +515,7 @@
 def annealing(labels, particles, grain_class, class_energy):
     out = jax.ShapeDtypeStruct((1, ORDERS, ROWS, 16, 256), jnp.float32)
     arguments = [labels, particles, grain_class.reshape(1, -1), class_energy]
-    return pl.pallas_call(
+    made = pl.pallas_call(
         annealing_kernel,
         out_shape=(out, out),
         in_specs=[pl.BlockSpec(memory_space=pltpu.HBM)] * 4,
@@ -491,6 +540,7 @@
         ),
         name="annealing",
     )(*(pltpu.with_memory_space_constraint(a, pltpu.HBM) for a in arguments))
+    return tuple(part * (1.0 / ROOT2) for part in made)
 
 
 def solution(mesh):

time: 24.3 us -> 21.1 us (0.87)
  the two profiles are of different devices: /device:TPU:255 before, /device:TPU:1 now
where the time goes in v3:
time: 21.1 us; the launch traced here: 20.9 us
  Pallas kernels  19.2 us (91%)
  other arithmetic  1.09 us (5%)
  between operations  0.64 us (3%)
    pallas_call x1, Pallas kernels, annealing(): pl.pallas_call(annealing_kernel, out_shape=(out, out), in_specs=[pl.Block...  19.2 us
    mul x1, other arithmetic, annealing(): return tuple((part * (1.0 / ROOT2) for part in made))  1.09 us

profile of v3, /device:TPU:1, one launch (start us, length us, event | category | flops | bytes accessed | tf_op | source)
XLA Modules:
  0.0 20.9 jit_solution(2431428023574402338)
XLA Ops:
  0.6 19.2 %annealing.1 = (f32[1,8,4,16,256]{4,3,2,1,0:T(8,128)S(1)}, f32[1,8,4,16,256]{4,3,2,1,0:T(8,128)S(1)}) custom-call(s32[4,16,256]{2,1,0:T(8,128)} %lab_hbm.1, s32[4,16,256]{2,1,0:T(8,128)} %msk_hbm.1, s32[1,128]{1,0:T(1,128)} %bitcast.1, f32[4]{0:T(128)} %energy_hbm.1), custom_call_target="tpu_custom_call" | custom-call | tf_op jit(solution)/shard_map/annealing/pallas_call | solution.py:518
  19.9 1.1 %broadcast_multiply_fusion = (f32[1,8,4,16,256]{4,3,2,1,0:T(8,128)}, f32[1,8,4,16,256]{4,3,2,1,0:T(8,128)}) fusion(f32[1,8,4,16,256]{4,3,2,1,0:T(8,128)S(1)} %get-tuple-element.5, f32[1,8,4,16,256]{4,3,2,1,0:T(8,128)S(1)} %get-tuple-element.4), kind=kLoop, calls=%fused_computation | loop fusion | flops 262144 | bytes 2097152 | tf_op jit(solution)/shard_map/mul | solution.py:543

commit v4 on v3

--- a/solution.py
+++ b/solution.py
@@ -126,49 +126,74 @@
     for copy in local_copies + table_copies:
         copy.start()
 
-    def partner(distance):
-        crossed = jnp.where(jnp.logical_or(place + distance < 0, place + distance > 3), 1, 0)
-        half = lax.rem(tm // 2 + crossed, 2)
-        return half * 2 + lax.rem(tm, 2), lax.rem(me + distance + count, count)
-
     odd = lax.rem(tm, 2) == 1
+
+    def away(distance, holder):
+        return holder, lax.rem(me + distance + count, count)
+
+    def crosses(distance):
+        return jnp.logical_or(place + distance < 0, place + distance > 3)
+
+    def across(distance):
+        sends = jnp.logical_and(tm == 1, crosses(distance))
+        return jnp.logical_and(sends, place != 1) if distance == -2 else sends
 
     def greet(device):
         pl.semaphore_signal(barrier, inc=1, device_id=device, device_id_type=MESH)
 
     barrier = pltpu.get_barrier_semaphore()
-
-    @pl.when(odd)
-    def _():
-        for distance in (1, -1):
-            greet(partner(distance))
-
-    @pl.when(tm == 3)
-    def _():
-        for distance in (2, -2):
-            greet(partner(distance))
+    targets = 1
+    for distance in (1, -1, 2, -2):
+        one = abs(distance) == 1
+        greets = odd if one else tm == 3
+        if distance == 2:
+            greets = jnp.logical_and(greets, place != 3)
+        pl.when(greets)(
+            functools.partial(greet, away(distance, jnp.where(crosses(distance), 1, tm)))
+        )
+        straight = jnp.where(crosses(distance), tm == 1, tm >= (1 if one else 3))
+        if not one:
+            straight = jnp.logical_and(straight, tm == 3)
+        targets = targets + jnp.where(straight, 1, 0) + jnp.where(across(distance), 1, 0)
 
     @pl.when(jnp.logical_not(odd))
     def _():
         greet((tm + 1, me))
 
-    far = [partner(distance)[0] == 3 for distance in (2, -2)]
-
-    def halo(moves, sending, act):
-        for m in moves:
-            distance, least, array, arrays, first, rows, there = MOVES[m]
-            target = partner(distance)
+    def moved(m, over):
+        distance, _, array, arrays, first, rows, there = MOVES[m]
+        return pltpu.make_async_remote_copy(
+            src_ref=cells.at[pl.ds(array, arrays), :, pl.ds(first, rows)],
+            dst_ref=cells.at[pl.ds(array, arrays), :, pl.ds(there, rows)],
+            send_sem=send_sem.at[10 * over + m],
+            recv_sem=recv_sem.at[m],
+            device_id=away(distance, 3 if over else tm),
+            device_id_type=MESH,
+        )
+
+    def halo(act):
+        for m, (distance, least, *_) in enumerate(MOVES):
+            inside = jnp.logical_or(tm == 1, jnp.logical_not(crosses(distance)))
+            wanted = jnp.logical_and(jnp.logical_and(odd, tm >= least), inside)
+            pl.when(wanted)(functools.partial(act, moved(m, 0)))
+            pl.when(across(distance))(functools.partial(act, moved(m, 1)))
+
+    def relay(act):
+        for m in (3, 5):
+            _, _, array, arrays, first, rows, there = MOVES[m]
             copy = pltpu.make_async_remote_copy(
-                src_ref=cells.at[pl.ds(array, arrays), :, pl.ds(first, rows)],
+                src_ref=cells.at[pl.ds(array, arrays), :, pl.ds(first + ROWS, rows)],
                 dst_ref=cells.at[pl.ds(array, arrays), :, pl.ds(there, rows)],
-                send_sem=send_sem.at[m],
+                send_sem=send_sem.at[13 + m],
                 recv_sem=recv_sem.at[m],
-                device_id=target,
+                device_id=away(-1, 3),
                 device_id_type=MESH,
             )
-            receiver = target[0] if sending else tm
-            wanted = jnp.logical_and(odd, receiver >= least)
-            pl.when(wanted)(functools.partial(act, copy))
+            pl.when(jnp.logical_and(tm == 1, place == 0))(functools.partial(act, copy))
+
+    def halo_received(moves):
+        for m in moves:
+            pl.when(jnp.logical_and(odd, tm >= MOVES[m][1]))(moved(m, 0).wait_recv)
 
     def hand(copies, sending, act):
         for h in copies:
@@ -193,9 +218,9 @@
 
     @pl.when(odd)
     def _():
-        pl.semaphore_wait(barrier, 3 + jnp.where(far[0], 1, 0) + jnp.where(far[1], 1, 0))
-
-    halo(range(6), True, start)
+        pl.semaphore_wait(barrier, targets)
+
+    halo(start)
 
     for copy in table_copies:
         copy.wait()
@@ -445,7 +470,7 @@
     unpack(HALO, ROWS)
     pairs(HALO, ROWS // 2, prepare)
 
-    low_late = jnp.logical_or(place < 2, me == 2)
+    low_late = place < 2
 
     def split(level, phase, lo, hi):
         reach = by_slice(tm, REACH[level])
@@ -465,7 +490,9 @@
         for side, (halos, far_halos, hands, far_hands) in enumerate(SIDES):
             @pl.when(at_low if side == 0 else jnp.logical_not(at_low))
             def _():
-                halo(halos, False, received)
+                halo_received(halos)
+                if side == 1:
+                    relay(start)
                 hand(hands, True, start)
                 hand(hands, False, received)
         first = jnp.where(at_low, HALO - 4, HALO + ROWS)
@@ -474,7 +501,7 @@
         for side, (halos, far_halos, hands, far_hands) in enumerate(SIDES):
             @pl.when(at_low if side == 0 else jnp.logical_not(at_low))
             def _():
-                halo(far_halos, False, received)
+                halo_received(far_halos)
                 hand(far_hands, True, start)
                 hand(far_hands, False, received)
 
@@ -505,7 +532,8 @@
     write(d3, 2, 3)
     level_of("6", level6)
     write(e4, 3, -1)
-    halo(range(6), True, sent)
+    halo(sent)
+    relay(sent)
     hand(range(6), True, sent)
     for which in (0, 1):
         for copy in sends(which):
@@ -526,7 +554,7 @@
             pltpu.SMEM((4,), jnp.float32),
             pltpu.VMEM((2, 2, ORDERS, ROWS + 2, 16, 128), jnp.float32),
             pltpu.SemaphoreType.DMA((6,)),
-            pltpu.SemaphoreType.DMA((10,)),
+            pltpu.SemaphoreType.DMA((20,)),
             pltpu.SemaphoreType.DMA((10,)),
             pltpu.SemaphoreType.DMA((4,)),
             pltpu.VMEM((256, 256), jnp.bfloat16),

time: 21.1 us -> 20.5 us (0.972)
  the two profiles are of different devices: /device:TPU:1 before, /device:TPU:255 now
where the time goes in v4:
time: 20.5 us; the launch traced here: 20.3 us
  Pallas kernels  18.5 us (90%)
  other arithmetic  1.09 us (5%)
  between operations  0.64 us (3%)
    pallas_call x1, Pallas kernels, annealing(): pl.pallas_call(annealing_kernel, out_shape=(out, out), in_specs=[pl.Block...  18.5 us
    mul x1, other arithmetic, annealing(): return tuple((part * (1.0 / ROOT2) for part in made))  1.09 us

profile of v4, /device:TPU:255, one launch (start us, length us, event | category | flops | bytes accessed | tf_op | source)
XLA Modules:
  0.0 20.3 jit_solution(5372621145730941225)
XLA Ops:
  0.6 18.5 %annealing.1 = (f32[1,8,4,16,256]{4,3,2,1,0:T(8,128)S(1)}, f32[1,8,4,16,256]{4,3,2,1,0:T(8,128)S(1)}) custom-call(s32[4,16,256]{2,1,0:T(8,128)} %lab_hbm.1, s32[4,16,256]{2,1,0:T(8,128)} %msk_hbm.1, s32[1,128]{1,0:T(1,128)} %bitcast.1, f32[4]{0:T(128)} %energy_hbm.1), custom_call_target="tpu_custom_call" | custom-call | tf_op jit(solution)/shard_map/annealing/pallas_call | solution.py:546
  19.2 1.1 %broadcast_multiply_fusion = (f32[1,8,4,16,256]{4,3,2,1,0:T(8,128)}, f32[1,8,4,16,256]{4,3,2,1,0:T(8,128)}) fusion(f32[1,8,4,16,256]{4,3,2,1,0:T(8,128)S(1)} %get-tuple-element.5, f32[1,8,4,16,256]{4,3,2,1,0:T(8,128)S(1)} %get-tuple-element.4), kind=kLoop, calls=%fused_computation | loop fusion | flops 262144 | bytes 2097152 | tf_op jit(solution)/shard_map/mul | solution.py:571

commit v5 on v4

--- a/solution.py
+++ b/solution.py
@@ -173,10 +173,11 @@
 
     def halo(act):
         for m, (distance, least, *_) in enumerate(MOVES):
+            pl.when(across(distance))(functools.partial(act, moved(m, 1)))
+        for m, (distance, least, *_) in enumerate(MOVES):
             inside = jnp.logical_or(tm == 1, jnp.logical_not(crosses(distance)))
             wanted = jnp.logical_and(jnp.logical_and(odd, tm >= least), inside)
             pl.when(wanted)(functools.partial(act, moved(m, 0)))
-            pl.when(across(distance))(functools.partial(act, moved(m, 1)))
 
     def relay(act):
         for m in (3, 5):
@@ -216,11 +217,13 @@
     for copy in local_copies:
         copy.wait()
 
-    @pl.when(odd)
-    def _():
+    early = jnp.logical_and(tm == 1, place == 0)
+
+    def depart():
         pl.semaphore_wait(barrier, targets)
-
-    halo(start)
+        halo(start)
+
+    pl.when(jnp.logical_and(odd, jnp.logical_not(early)))(depart)
 
     for copy in table_copies:
         copy.wait()
@@ -469,6 +472,7 @@
     send(-1, 0)
     unpack(HALO, ROWS)
     pairs(HALO, ROWS // 2, prepare)
+    pl.when(early)(depart)
 
     low_late = place < 2
 

time: 20.5 us -> 20.9 us (1.020)
  the two profiles are of different devices: /device:TPU:255 before, /device:TPU:161 now
where the time goes in v5:
time: 20.9 us; the launch traced here: 20.8 us
  Pallas kernels  19 us (91%)
  other arithmetic  1.09 us (5%)
  between operations  0.64 us (3%)
    pallas_call x1, Pallas kernels, annealing(): pl.pallas_call(annealing_kernel, out_shape=(out, out), in_specs=[pl.Block...  19 us
    mul x1, other arithmetic, annealing(): return tuple((part * (1.0 / ROOT2) for part in made))  1.09 us

profile of v5, /device:TPU:161, one launch (start us, length us, event | category | flops | bytes accessed | tf_op | source)
XLA Modules:
  0.0 20.8 jit_solution(17096445828526356723)
XLA Ops:
  0.6 19.0 %annealing.1 = (f32[1,8,4,16,256]{4,3,2,1,0:T(8,128)S(1)}, f32[1,8,4,16,256]{4,3,2,1,0:T(8,128)S(1)}) custom-call(s32[4,16,256]{2,1,0:T(8,128)} %lab_hbm.1, s32[4,16,256]{2,1,0:T(8,128)} %msk_hbm.1, s32[1,128]{1,0:T(1,128)} %bitcast.1, f32[4]{0:T(128)} %energy_hbm.1), custom_call_target="tpu_custom_call" | custom-call | tf_op jit(solution)/shard_map/annealing/pallas_call | solution.py:550
  19.7 1.1 %broadcast_multiply_fusion = (f32[1,8,4,16,256]{4,3,2,1,0:T(8,128)}, f32[1,8,4,16,256]{4,3,2,1,0:T(8,128)}) fusion(f32[1,8,4,16,256]{4,3,2,1,0:T(8,128)S(1)} %get-tuple-element.5, f32[1,8,4,16,256]{4,3,2,1,0:T(8,128)S(1)} %get-tuple-element.4), kind=kLoop, calls=%fused_computation | loop fusion | flops 262144 | bytes 2097152 | tf_op jit(solution)/shard_map/mul | solution.py:575
